TPU v7x, 256 devices: a whole 4x4x8 slice. The times are simulated.
256 devices in a mesh: expert: 64 (over z, y, core), dp: 4 (over x).
Axes of the slice: x: 4, y: 4, z: 8, core: 2. Of those that a mesh axis runs over, the one named last changes fastest.
Arguments:
- tokens: bfloat16 [8192, 4096], P('expert', 'dp'), may hold values from -6 to 6
- to_latent: bfloat16 [4096, 1024], P('dp'), may hold values from -0.09375 to 0.09375
- from_latent: bfloat16 [1024, 4096], P(None, 'dp'), may hold values from -0.1875 to 0.1875
- expert_gate: bfloat16 [64, 1024, 2048], P('expert', None, 'dp'), may hold values from -0.1875 to 0.1875
- expert_up: bfloat16 [64, 1024, 2048], P('expert', None, 'dp'), may hold values from -0.1875 to 0.1875
- expert_down: bfloat16 [64, 2048, 1024], P('expert', 'dp'), may hold values from -0.125 to 0.125
- routes: int32 [8192, 8], P('expert'), may hold values from 0 to 63, as said below
- slot_index: int32 [8192, 8], P('expert'), may hold values from 0 to 20, as said below
- route_gates: float32 [8192, 8], P('expert'), may hold values from 0.05 to 0.5
- grad_output: bfloat16 [8192, 4096], P('expert', 'dp'), may hold values from -6 to 6
Outputs:
- layer_output: bfloat16 [8192, 4096], P('expert', 'dp')
- grad_tokens: bfloat16 [8192, 4096], P('expert', 'dp')
- grad_to_latent: float32 [1024, 4096], P('expert', 'dp')
- grad_from_latent: float32 [1024, 4096], P('expert', 'dp')
- grad_gate: bfloat16 [64, 1024, 2048], P('expert', None, 'dp')
- grad_up: bfloat16 [64, 1024, 2048], P('expert', None, 'dp')
- grad_down: bfloat16 [64, 2048, 1024], P('expert', 'dp')
Inputs may be any that keep to these rules, and one draw needn't show every extreme that they name: `routes`: each row names 8 different experts. `slot_index`: among the routes of one device (aligned blocks of 128 rows) that name the same expert, slots count 0, 1, 2, ... in an order of that device's routes drawn from the seed; routes past the capacity hold 20 and are dropped. On every device some expert is named by more than 20 rows.
All inputs are finite; a program needn't handle non-finite values.
Results may differ from a plain program's by a relative error of at most 0.03.
Values may be sent and summed in bfloat16 or wider, within the bound.
A program may use at most 128 MiB of HBM per device.

v0:
```python
import jax
import jax.numpy as jnp
from jax import lax
from jax.sharding import PartitionSpec as P


def dp_total(summand):
    return lax.psum(summand.astype(jnp.bfloat16), "dp").astype(jnp.float32)


def send_rows(row_block):
    return lax.all_to_all(row_block, "expert", split_axis=0, concat_axis=0, tiled=True)


def return_rows(partial_value, routes, slot_index, capacity):
    latent_width = partial_value.shape[2]
    kept_routes = slot_index < capacity
    arrived = lax.all_to_all(
        partial_value, "expert", split_axis=0, concat_axis=0, tiled=True
    ).astype(jnp.float32)
    places = jnp.where(kept_routes, routes * capacity + slot_index, arrived.shape[0] * capacity)
    flat_rows = jnp.concatenate(
        [arrived.reshape(-1, latent_width), jnp.zeros((1, latent_width), jnp.float32)], axis=0
    )
    return flat_rows[places]


def spread_grad(left_side, right_side, scaling):
    return lax.psum_scatter(
        lax.dot_general(
            left_side, right_side, (((0,), (0,)), ((), ())), preferred_element_type=jnp.float32
        )
        * scaling,
        "expert",
        scatter_dimension=0,
        tiled=True,
    )


def local(
    tokens,
    to_latent,
    from_latent,
    expert_gate,
    expert_up,
    expert_down,
    routes,
    slot_index,
    route_gates,
    grad_output,
):
    contract_last = (((1,), (1,)), ((), ()))
    contract_first = (((0,), (0,)), ((), ()))
    expert_count = lax.axis_size("expert")
    dp_count = lax.axis_size("dp")
    token_count, route_count = routes.shape
    latent_width = to_latent.shape[1]
    capacity = dp_count * max(
        1,
        min(
            token_count // (4 * dp_count),
            5 * token_count * route_count // (4 * expert_count * dp_count),
        ),
    )
    scaling = (token_count * expert_count) ** (-0.5)
    total_cells = expert_count * capacity
    kept_routes = slot_index < capacity
    cell_index = jnp.where(kept_routes, routes * capacity + slot_index, total_cells)
    entries = jnp.full((total_cells + 1,), token_count * route_count, jnp.int32)
    entries = entries.at[cell_index.reshape(-1)].set(
        jnp.arange(token_count * route_count, dtype=jnp.int32)
    )[:total_cells]
    latent = dp_total(jnp.dot(tokens, to_latent, preferred_element_type=jnp.float32)).astype(
        jnp.bfloat16
    )
    latent_pad = jnp.concatenate([latent, jnp.zeros((1, latent_width), jnp.bfloat16)], axis=0)
    outgoing = latent_pad[entries // route_count].reshape(expert_count, capacity, latent_width)
    received = send_rows(outgoing).reshape(-1, latent_width)
    gate_mat = expert_gate[0]
    up_mat = expert_up[0]
    down_mat = expert_down[0]
    pre_gate = jnp.dot(received, gate_mat, preferred_element_type=jnp.float32)
    pre_up = jnp.dot(received, up_mat, preferred_element_type=jnp.float32)
    sigmoid_gate = jax.nn.sigmoid(pre_gate)
    activated = pre_gate * sigmoid_gate
    hidden = (activated * pre_up).astype(jnp.bfloat16)
    partial_value = jnp.dot(hidden, down_mat, preferred_element_type=jnp.float32).astype(
        jnp.bfloat16
    )
    picked = return_rows(
        partial_value.reshape(expert_count, capacity, latent_width), routes, slot_index, capacity
    )
    mixed_latent = dp_total(jnp.einsum("tk,tkl->tl", route_gates, picked)).astype(jnp.bfloat16)
    layer_output = jnp.dot(mixed_latent, from_latent, preferred_element_type=jnp.float32).astype(
        jnp.bfloat16
    )
    mixed_grad = dp_total(
        lax.dot_general(grad_output, from_latent, contract_last, preferred_element_type=jnp.float32)
    ).astype(jnp.bfloat16)
    grad_from_latent = spread_grad(mixed_latent, grad_output, scaling)
    route_grads = (route_gates[:, :, None] * mixed_grad.astype(jnp.float32)[:, None, :]).astype(
        jnp.bfloat16
    )
    grad_pad = jnp.concatenate(
        [route_grads.reshape(-1, latent_width), jnp.zeros((1, latent_width), jnp.bfloat16)], axis=0
    )
    grad_received = send_rows(
        grad_pad[entries].reshape(expert_count, capacity, latent_width)
    ).reshape(-1, latent_width)
    grad_hidden = lax.dot_general(
        grad_received, down_mat, contract_last, preferred_element_type=jnp.float32
    )
    grad_pre_gate = (
        grad_hidden * pre_up * (sigmoid_gate * (1.0 + pre_gate * (1.0 - sigmoid_gate)))
    ).astype(jnp.bfloat16)
    grad_pre_up = (grad_hidden * activated).astype(jnp.bfloat16)
    grad_expert_rows = lax.dot_general(
        grad_pre_gate, gate_mat, contract_last, preferred_element_type=jnp.float32
    )
    grad_expert_rows = (
        grad_expert_rows
        + lax.dot_general(grad_pre_up, up_mat, contract_last, preferred_element_type=jnp.float32)
    ).astype(jnp.bfloat16)
    grad_gate = (
        lax.dot_general(received, grad_pre_gate, contract_first, preferred_element_type=jnp.float32)
        * scaling
    ).astype(jnp.bfloat16)[None]
    grad_up = (
        lax.dot_general(received, grad_pre_up, contract_first, preferred_element_type=jnp.float32)
        * scaling
    ).astype(jnp.bfloat16)[None]
    grad_down = (
        lax.dot_general(hidden, grad_received, contract_first, preferred_element_type=jnp.float32)
        * scaling
    ).astype(jnp.bfloat16)[None]
    back_picked = return_rows(
        grad_expert_rows.reshape(expert_count, capacity, latent_width), routes, slot_index, capacity
    )
    grad_latent = dp_total(jnp.sum(back_picked, axis=1)).astype(jnp.bfloat16)
    grad_tokens = lax.dot_general(
        grad_latent, to_latent, contract_last, preferred_element_type=jnp.float32
    ).astype(jnp.bfloat16)
    grad_to_latent = spread_grad(grad_latent, tokens, scaling)
    return (
        layer_output,
        grad_tokens,
        grad_to_latent,
        grad_from_latent,
        grad_gate,
        grad_up,
        grad_down,
    )


def solution(mesh):
    return jax.shard_map(
        local,
        mesh=mesh,
        in_specs=(
            P("expert", "dp"),
            P("dp", None),
            P(None, "dp"),
            P("expert", None, "dp"),
            P("expert", None, "dp"),
            P("expert", "dp", None),
            P("expert", None),
            P("expert", None),
            P("expert", None),
            P("expert", "dp"),
        ),
        out_specs=(
            P("expert", "dp"),
            P("expert", "dp"),
            P("expert", "dp"),
            P("expert", "dp"),
            P("expert", None, "dp"),
            P("expert", None, "dp"),
            P("expert", "dp", None),
        ),
        check_vma=False,
    )
```

profile of v0, /device:TPU:1, one launch (start us, length us, event | category | flops | bytes accessed | tf_op | source)
XLA Modules:
  0.0 784.2 jit_solution(13858006009804351855)
XLA Ops:
  7.2 0.0 all-reduce.11.cloned.1.call-start
  7.3 3.0 convolution_convert_fusion.4
  10.2 1.5 convolution_convert_fusion.2
  11.8 0.0 all-reduce.11.cloned.1.call-update
  11.8 0.1 copy.17
  11.9 0.1 reshape.77
  12.1 4.3 scatter_custom_fusion
  16.4 45.3 %all-reduce.11.cloned.1.call-done = (bf16[128,1024]{1,0:T(8,128)(2,1)}, bf16[128,1024]{1,0:T(8,128)(2,1)}) async-done(((bf16[128,1024]{1,0:T(8,128)(2,1)}, bf16[128,1024]{1,0:T(8,128)(2,1)}), (bf16[128,1024]{1,0:T(8,128)(2,1)}, bf16[128,1024]{1,0:T(8,128)(2,1)})) %all-reduce.11.cloned.1.call-update) | async-done | bytes 524304 | tf_op jit(solution)/shard_map/psum | solution.py:8
  61.8 1.0 concatenate.16
  62.7 5.1 gather_fusion
  67.8 5.1 reshape.78
  73.0 13.1 %all-to-all-start = ((bf16[64,20,1024]{2,1,0:T(8,128)(2,1)}), bf16[64,20,1024]{2,1,0:T(8,128)(2,1)}, u32[]{:S(2)}, u32[]{:S(2)}) async-start(bf16[64,20,1024]{2,1,0:T(8,128)(2,1)} %reshape.78), calls=%async_computation | async-start | bytes 6291456 | tf_op jit(solution)/shard_map/all_to_all | solution.py:12
  86.1 0.1 copy.19
  86.2 0.1 mul.65
  86.4 0.3 fusion
  86.7 1.6 concatenate.19
  88.3 8.6 %gather_fusion.1 = bf16[1280,1024]{1,0:T(8,128)(2,1)} fusion(bf16[1025,1024]{1,0:T(8,128)(2,1)} %concatenate.19, s32[2048]{0:T(1024)S(1)} %pad_clamp_fusion), kind=kCustom, calls=%fused_computation.1 | custom fusion | bytes 5248000 | tf_op jit(solution)/shard_map/gather | solution.py:108
  96.8 5.2 reshape.82
  102.0 56.6 %all-to-all-done = bf16[64,20,1024]{2,1,0:T(8,128)(2,1)} async-done(((bf16[64,20,1024]{2,1,0:T(8,128)(2,1)}), bf16[64,20,1024]{2,1,0:T(8,128)(2,1)}, u32[]{:S(2)}, u32[]{:S(2)}) %all-to-all-start) | async-done | bytes 2621472 | tf_op jit(solution)/shard_map/all_to_all | solution.py:12
  158.6 6.8 all-to-all-start.2
  165.4 5.3 reshape.79
  170.7 4.9 fusion.11
  175.6 3.0 fusion.15
  178.6 59.4 %all-to-all-done.2 = bf16[64,20,1024]{2,1,0:T(8,128)(2,1)} async-done(((bf16[64,20,1024]{2,1,0:T(8,128)(2,1)}), bf16[64,20,1024]{2,1,0:T(8,128)(2,1)}, u32[]{:S(2)}, u32[]{:S(2)}) %all-to-all-start.2) | async-done | bytes 2621472 | tf_op jit(solution)/shard_map/all_to_all | solution.py:12
  238.0 5.2 reshape.83
  243.2 7.3 multiply_convert_fusion
  250.5 1.1 copy-done.4
  251.6 3.0 convolution_convert_fusion
  254.6 5.1 reshape.80
  259.8 6.7 all-to-all-start.1
  266.5 3.3 fusion.13
  269.7 3.1 add_convert_fusion
  272.8 5.2 reshape.84
  278.0 61.1 %all-to-all-done.1 = bf16[64,20,1024]{2,1,0:T(8,128)(2,1)} async-done(((bf16[64,20,1024]{2,1,0:T(8,128)(2,1)}), bf16[64,20,1024]{2,1,0:T(8,128)(2,1)}, u32[]{:S(2)}, u32[]{:S(2)}) %all-to-all-start.1) | async-done | bytes 2621472 | tf_op jit(solution)/shard_map/all_to_all | solution.py:18
  339.1 6.7 all-to-all-start.3
  345.8 0.3 all-reduce.9.cloned.1.call-start
  346.1 0.1 copy.18
  346.2 0.1 reshape.112
  346.2 0.1 copy.20
  346.4 5.2 reshape.81
  351.6 3.5 concatenate.17
  355.1 8.1 %gather_fusion.3 = bf16[1024,1024]{1,0:T(8,128)(2,1)} fusion(bf16[1281,1024]{1,0:T(8,128)(2,1)} %concatenate.17, s32[1024]{0:T(1024)S(1)} %broadcast_clamp_fusion), kind=kCustom, calls=%fused_computation.3 | custom fusion | bytes 4198400 | tf_op jit(solution)/shard_map/gather | solution.py:25
  363.2 2.3 fusion.2
  365.5 0.8 copy.23
  366.3 52.1 %all-to-all-done.3 = bf16[64,20,1024]{2,1,0:T(8,128)(2,1)} async-done(((bf16[64,20,1024]{2,1,0:T(8,128)(2,1)}), bf16[64,20,1024]{2,1,0:T(8,128)(2,1)}, u32[]{:S(2)}, u32[]{:S(2)}) %all-to-all-start.3) | async-done | bytes 2621472 | tf_op jit(solution)/shard_map/all_to_all | solution.py:18
  418.4 5.2 reshape.85
  423.6 4.7 pad_convert_fusion
  428.3 8.9 %gather_fusion.2 = f32[1024,1024]{1,0:T(8,128)} fusion(f32[1281,1024]{1,0:T(8,128)} %pad_convert_fusion, s32[1024]{0:T(1024)S(1)} %broadcast_clamp_fusion), kind=kCustom, calls=%fused_computation.2 | custom fusion | bytes 8392704 | tf_op jit(solution)/shard_map/gather | solution.py:25
  437.3 4.0 bitcast_reduce_fusion
  441.2 0.0 all-reduce.9.cloned.1.call-update
  441.3 0.0 reduce-scatter.3.cloned.1.call-start
  441.3 42.6 %all-reduce.9.cloned.1.call-done = (bf16[128,1024]{1,0:T(8,128)(2,1)}, bf16[128,1024]{1,0:T(8,128)(2,1)}) async-done(((bf16[128,1024]{1,0:T(8,128)(2,1)}, bf16[128,1024]{1,0:T(8,128)(2,1)}), (bf16[128,1024]{1,0:T(8,128)(2,1)}, bf16[128,1024]{1,0:T(8,128)(2,1)})) %all-reduce.9.cloned.1.call-update) | async-done | bytes 524304 | tf_op jit(solution)/shard_map/psum | solution.py:8
  483.9 3.7 convolution_multiply_fusion.1
  487.6 0.0 reduce-scatter.3.cloned.1.call-update
  487.7 0.0 reduce-scatter.5.cloned.1.call-start
  487.7 3.8 convolution_multiply_fusion
  491.5 4.8 fusion.6
  496.3 2.5 fusion.5
  498.9 2.5 fusion.4
  501.4 1.2 convolution_convert_fusion.3
  502.5 0.6 copy-done.1
  503.1 1.5 convolution_convert_fusion.1
  504.6 125.7 %reduce-scatter.3.cloned.1.call-done = f32[16,1024]{1,0:T(8,128)} async-done(((f32[1024,1024]{1,0:T(8,128)}), f32[16,1024]{1,0:T(8,128)}) %reduce-scatter.3.cloned.1.call-update) | async-done | bytes 65552 | tf_op jit(solution)/shard_map/reduce_scatter | solution.py:29
  630.3 147.4 %reduce-scatter.5.cloned.1.call-done = f32[16,1024]{1,0:T(8,128)} async-done(((f32[1024,1024]{1,0:T(8,128)}), f32[16,1024]{1,0:T(8,128)}) %reduce-scatter.5.cloned.1.call-update) | async-done | bytes 65552 | tf_op jit(solution)/shard_map/reduce_scatter | solution.py:29
  (41 shorter events, 0.2 us)
Async XLA Ops:
  7.2 3.1 copy-start
  7.2 3.1 copy-start.7
  7.2 4.6 copy-start.12
  7.2 4.6 copy-start.13
  7.2 54.6 %all-reduce.11.cloned.1.call-start = ((), (), s32[]{:S(2)}) async-start(), calls=%async_computation.9 | async-start | bytes 1048576 | tf_op jit(solution)/shard_map/psum | solution.py:8
  73.0 13.1 %copy-start.11 = (f32[128,8]{0,1:T(8,128)S(1)}, f32[128,8]{0,1:T(8,128)}, u32[]{:S(2)}) copy-start(f32[128,8]{0,1:T(8,128)} %param.18) | copy-start | bytes 12292
  73.0 13.3 %copy-start.10 = (bf16[128,1024]{1,0:T(8,128)(2,1)S(1)}, bf16[128,1024]{1,0:T(8,128)(2,1)}, u32[]{:S(2)}) copy-start(bf16[128,1024]{1,0:T(8,128)(2,1)} %get-tuple-element.10) | copy-start | bytes 786436
  73.0 85.6 %all-to-all-start = ((bf16[64,20,1024]{2,1,0:T(8,128)(2,1)}), bf16[64,20,1024]{2,1,0:T(8,128)(2,1)}, u32[]{:S(2)}, u32[]{:S(2)}) async-start(bf16[64,20,1024]{2,1,0:T(8,128)(2,1)} %reshape.78), calls=%async_computation | async-start | bytes 6291456 | tf_op jit(solution)/shard_map/all_to_all | solution.py:12
  158.6 79.4 %all-to-all-start.2 = ((bf16[64,20,1024]{2,1,0:T(8,128)(2,1)}), bf16[64,20,1024]{2,1,0:T(8,128)(2,1)}, u32[]{:S(2)}, u32[]{:S(2)}) async-start(bf16[64,20,1024]{2,1,0:T(8,128)(2,1)} %reshape.82), calls=%async_computation.2 | async-start | bytes 6291456 | tf_op jit(solution)/shard_map/all_to_all | solution.py:12
  165.4 5.3 copy-start.5
  170.7 4.9 copy-start.2
  170.7 4.9 copy-start.15
  243.2 8.4 %copy-start.14 = (bf16[1,512,1024]{2,1,0:T(8,128)(2,1)S(1)}, bf16[1,512,1024]{2,1,0:T(8,128)(2,1)}, u32[]{:S(2)}) copy-start(bf16[1,512,1024]{2,1,0:T(8,128)(2,1)} %param.15) | copy-start | bytes 3145732
  250.5 1.1 copy-start.4
  259.8 79.3 %all-to-all-start.1 = ((bf16[64,20,1024]{2,1,0:T(8,128)(2,1)}), bf16[64,20,1024]{2,1,0:T(8,128)(2,1)}, u32[]{:S(2)}, u32[]{:S(2)}) async-start(bf16[64,20,1024]{2,1,0:T(8,128)(2,1)} %reshape.80), calls=%async_computation.1 | async-start | bytes 6291456 | tf_op jit(solution)/shard_map/all_to_all | solution.py:18
  266.5 3.3 copy-start.6
  339.1 79.3 %all-to-all-start.3 = ((bf16[64,20,1024]{2,1,0:T(8,128)(2,1)}), bf16[64,20,1024]{2,1,0:T(8,128)(2,1)}, u32[]{:S(2)}, u32[]{:S(2)}) async-start(bf16[64,20,1024]{2,1,0:T(8,128)(2,1)} %reshape.84), calls=%async_computation.3 | async-start | bytes 6291456 | tf_op jit(solution)/shard_map/all_to_all | solution.py:18
  345.8 138.2 %all-reduce.9.cloned.1.call-start = ((), (), s32[]{:S(2)}) async-start(), calls=%async_computation.8 | async-start | bytes 1048576 | tf_op jit(solution)/shard_map/psum | solution.py:8
  441.3 189.0 %reduce-scatter.3.cloned.1.call-start = ((), (), s32[]{:S(2)}) async-start(), calls=%async_computation.6 | async-start | bytes 4259840 | tf_op jit(solution)/shard_map/reduce_scatter | solution.py:29
  487.7 290.0 %reduce-scatter.5.cloned.1.call-start = ((), (), s32[]{:S(2)}) async-start(), calls=%async_computation.7 | async-start | bytes 4259840 | tf_op jit(solution)/shard_map/reduce_scatter | solution.py:29
  491.5 4.8 copy-start.3
  496.3 2.5 copy-start.16
  498.9 2.5 copy-start.9
  501.4 1.7 copy-start.1
  501.4 1.7 copy-start.8
Sparse Core Ops, SparseCore 0:
  11.9 49.8 all-reduce.10
  441.4 42.5 all-reduce.8
  488.6 141.6 reduce-scatter.2
  635.4 142.2 reduce-scatter.4
where the time goes:
time: 790 us; the launch traced here: 784 us
  waiting for transfers between devices  590 us (75%)
  local copies, waits for them, and re-layouts  85.7 us (11%)
  matrix products  51.4 us (7%)
  starting transfers between devices  33.7 us (4%)
  between operations  14 us (2%)
  other arithmetic  9.1 us (1%)
    reduce_scatter x2, waiting for transfers between devices, spread_grad(): lax.psum_scatter(lax.dot_general(left_side, right_side, (((0,), (0,)), ((...  273 us
    all_to_all x2, waiting for transfers between devices, send_rows(): lax.all_to_all(row_block, 'expert', split_axis=0, concat_axis=0, tiled=True)  116 us
    all_to_all x2, waiting for transfers between devices, return_rows(): lax.all_to_all(partial_value, 'expert', split_axis=0, concat_axis=0, tile...  113 us
    psum x2, waiting for transfers between devices, dp_total(): return lax.psum(summand.astype(jnp.bfloat16), 'dp').astype(jnp.float32)  88 us
    all_to_all x2, starting transfers between devices, send_rows(): lax.all_to_all(row_block, 'expert', split_axis=0, concat_axis=0, tiled=True)  19.9 us
    gather x2, local copies, waits for them, and re-layouts, return_rows(): return flat_rows[places]  17 us
  transfers between devices with their start and end apart: 8, of which 8 were waited for; matrix products, arithmetic and copies ran while one was open for 10% of the time, Pallas kernels for 0%

commit v1 on v0

v1 whole, which is shorter than its diff:
```python
import functools

import jax
import jax.numpy as jnp
from jax import lax
from jax.experimental import pallas as pl
from jax.experimental.pallas import tpu as pltpu
from jax.sharding import PartitionSpec as P

F32 = jnp.float32
BF16 = jnp.bfloat16
LAST = (((1,), (1,)), ((), ()))
FIRST = (((0,), (0,)), ((), ()))
MESH = pl.DeviceIdType.MESH


def remote(src, dst, send_sem, recv_sem, where):
    return pltpu.make_async_remote_copy(
        src_ref=src, dst_ref=dst, send_sem=send_sem, recv_sem=recv_sem, device_id=where, device_id_type=MESH
    )


def layer_kernel(
    cfg,
    routes_ref,
    slots_ref,
    gates_ref,
    tok_in,
    tl_in,
    fl_in,
    gate_in,
    up_in,
    down_in,
    go_in,
    lo_out,
    gt_out,
    gg_out,
    gu_out,
    gd_out,
    mixed_out,
    glat_out,
    tok_v,
    tl_v,
    fl_v,
    gate_v,
    up_v,
    down_v,
    go_v,
    lo_v,
    gt_v,
    gg_v,
    gu_v,
    gd_v,
    mixed_v,
    glat_v,
    xs_send_v,
    xs_recv_v,
    s_tab,
    g_tab,
    pp,
    pph,
    ppl,
    perm,
    outgoing,
    arrived,
    leaving,
    returned,
    full,
    part,
    relay,
    frm,
    pg_v,
    pu_v,
    hid_v,
    gpg_v,
    gpu_v,
    load_sem,
    store_sem,
    xs_ssem,
    xs_rsem,
    a2a_ssem,
    a2a_rsem,
    ag_ssem,
    ag_rsem,
    rs_ssem,
    rs_rsem,
    fin_ssem,
    fin_rsem,
):
    n, T, R, L, Q, W, G, NG, NC = (cfg[k] for k in ("n", "T", "R", "L", "Q", "W", "G", "NG", "NC"))
    scaling = cfg["scaling"]
    R2 = 2 * R
    RG = G * R
    RC = n * R // NC
    GC = NG // NC
    me = lax.axis_index("expert")
    x = lax.axis_index("dp")
    right = lax.rem(x + 1, 4)
    left = lax.rem(x + 3, 4)
    opp = lax.rem(x + 2, 4)
    peers = (right, left, opp)

    loads = [
        pltpu.make_async_copy(src, dst, load_sem.at[i])
        for i, (src, dst) in enumerate(
            (
                (tok_in, tok_v),
                (tl_in, tl_v),
                (go_in, go_v),
                (fl_in, fl_v),
                (gate_in.at[0], gate_v),
                (up_in.at[0], up_v),
                (down_in.at[0], down_v),
            )
        )
    ]
    for load in loads:
        load.start()
    barrier = pltpu.get_barrier_semaphore()
    for peer in peers:
        pl.semaphore_signal(barrier, inc=1, device_id={"dp": peer}, device_id_type=MESH)

    @pl.loop(1, n)
    def _(k):
        pl.semaphore_signal(barrier, inc=1, device_id={"expert": lax.rem(me + k, n)}, device_id_type=MESH)

    krel = lax.broadcasted_iota(jnp.int32, (n, T), 0)
    s_val = jnp.full((n, T), -1000, jnp.int32)
    g_val = jnp.zeros((n, T), F32)
    for j in range(routes_ref.shape[0]):
        rel = routes_ref[j : j + 1, :] - me
        rel = jnp.where(rel < 0, rel + n, rel)
        slot = slots_ref[j : j + 1, :]
        match = (krel == rel) & (slot < R)
        s_val = jnp.where(match, slot, s_val)
        g_val = jnp.where(match, gates_ref[j : j + 1, :], g_val)
    s_tab[...] = s_val
    g_tab[...] = g_val

    size = 4 * R2
    row = lax.broadcasted_iota(jnp.int32, (size, size), 0)
    col = lax.broadcasted_iota(jnp.int32, (size, size), 1)
    kk = jnp.where(row >= 2 * R2, jnp.where(row >= 3 * R2, 3, 2), jnp.where(row >= R2, 1, 0))
    rest = row - kk * R2
    half = jnp.where(rest >= R, 1, 0)
    perm[0] = jnp.where(col == half * (4 * R) + kk * R + rest - half * R, 1.0, 0.0).astype(BF16)
    kk = jnp.where(col >= 2 * R2, jnp.where(col >= 3 * R2, 3, 2), jnp.where(col >= R2, 1, 0))
    rest = col - kk * R2
    half = jnp.where(rest >= R, 1, 0)
    perm[1] = jnp.where(row == half * (4 * R) + kk * R + rest - half * R, 1.0, 0.0).astype(BF16)

    def xs_copy(ph, j):
        return remote(
            xs_send_v.at[ph, j], xs_recv_v.at[ph, x], xs_ssem.at[ph, j], xs_rsem.at[ph, x], {"dp": j}
        )

    def xs_start(ph, value):
        for j in range(4):
            xs_send_v[ph, j] = value[:, j * Q : (j + 1) * Q].astype(BF16)
        for peer in peers:
            xs_copy(ph, peer).start()

    def xs_finish(ph):
        total = xs_send_v[ph, x].astype(F32)
        for peer in peers:
            remote(
                xs_send_v.at[ph, x], xs_recv_v.at[ph, peer], xs_ssem.at[ph, peer], xs_rsem.at[ph, peer], {"dp": peer}
            ).wait_recv()
            total = total + xs_recv_v[ph, peer].astype(F32)
        total = total.astype(BF16)
        return jnp.concatenate([total[:, :W], total[:, W:]], axis=0)

    loads[0].wait()
    loads[1].wait()
    latent_part = jnp.dot(tok_v[...], tl_v[...], preferred_element_type=F32)
    pl.semaphore_wait(barrier, n - 1 + 3)
    xs_start(0, latent_part)
    loads[2].wait()
    loads[3].wait()
    xs_start(1, lax.dot_general(go_v[...], fl_v[...], LAST, preferred_element_type=F32))

    r_iota = lax.broadcasted_iota(jnp.int32, (G, R2, T), 1)

    @pl.loop(0, NG)
    def _(g):
        ks = pl.ds(pl.multiple_of(g * G, G), G)
        rows = pl.ds(pl.multiple_of(g * G * R2, G * R2), G * R2)
        s8 = jnp.broadcast_to(s_tab[ks, :].reshape(G, 1, T), (G, R2, T))
        g8 = jnp.broadcast_to(g_tab[ks, :].reshape(G, 1, T), (G, R2, T))
        g_hi = g8.astype(BF16).astype(F32)
        g_lo = g8 - g_hi
        for h in range(2):
            match = s8 == r_iota - h * R
            lanes = slice(h * T, (h + 1) * T)
            pp[rows, lanes] = jnp.where(match, 1.0, 0.0).reshape(G * R2, T).astype(BF16)
            pph[rows, lanes] = jnp.where(match, g_hi, 0.0).reshape(G * R2, T).astype(BF16)
            ppl[rows, lanes] = jnp.where(match, g_lo, 0.0).reshape(G * R2, T).astype(BF16)

    def dispatch(ph, stacked):
        @pl.loop(0, NG)
        def _(g):
            ks = pl.ds(pl.multiple_of(g * G, G), G)
            rows = pl.ds(pl.multiple_of(g * G * R2, G * R2), G * R2)
            if ph == 0:
                block = jnp.dot(pp[rows, :], stacked, preferred_element_type=F32)
            else:
                block = jnp.dot(pph[rows, :], stacked, preferred_element_type=F32)
                block = block + jnp.dot(ppl[rows, :], stacked, preferred_element_type=F32)
            outgoing[ph, ks] = block.reshape(G, R2, W).astype(BF16)

            @pl.loop(jnp.maximum(g * G, 1), g * G + G)
            def _(k):
                remote(
                    outgoing.at[ph, k],
                    arrived.at[ph, k],
                    a2a_ssem.at[ph],
                    a2a_rsem.at[ph, g],
                    {"expert": lax.rem(me + k, n)},
                ).start()

        arrived[ph, 0] = outgoing[ph, 0]

    dispatch(0, xs_finish(0))
    dispatch(1, xs_finish(1))

    def a2a_wait(ph, buf, g):
        @pl.when(g == 0)
        def _():
            pltpu.make_async_copy(buf.at[1:G], buf.at[1:G], a2a_rsem.at[ph, 0]).wait()

        @pl.when(g != 0)
        def _():
            ks = pl.ds(pl.multiple_of(g * G, G), G)
            pltpu.make_async_copy(buf.at[ks], buf.at[ks], a2a_rsem.at[ph, g]).wait()

    def group_rows(g):
        return pl.ds(pl.multiple_of(g * RG, RG), RG)

    halves = (slice(0, W), slice(W, 2 * W))

    def ag_copy(ph, g, kind, q):
        src = full.at[ph, q, group_rows(g)]
        if kind >= 2:
            src = full.at[ph, q, group_rows(g), halves[kind - 2]]
        where = {"dp": right if kind % 2 == 0 else left}
        return remote(src, src, ag_ssem.at[ph, g, kind], ag_rsem.at[ph, g, kind], where)

    def ag_start(ph, g):
        a2a_wait(ph, arrived.at[ph], g)
        for sub in range(G // 4):
            ks = pl.ds(pl.multiple_of(g * G + sub * 4, 4), 4)
            block = arrived[ph, ks].astype(F32).reshape(4 * R2, W).astype(BF16)
            dense = jnp.dot(perm[1], block, preferred_element_type=F32).astype(BF16)
            rows = pl.ds(pl.multiple_of(g * RG + sub * 4 * R, 4 * R), 4 * R)
            full[ph, x, rows, 0:W] = dense[: 4 * R]
            full[ph, x, rows, W : 2 * W] = dense[4 * R :]
        ag_copy(ph, g, 0, x).start()
        ag_copy(ph, g, 1, x).start()

    def ag_forward(ph, g):
        ag_copy(ph, g, 0, left).wait_recv()
        ag_copy(ph, g, 2, left).start()
        ag_copy(ph, g, 1, right).wait_recv()
        ag_copy(ph, g, 3, right).start()

    def ag_finish(ph, g):
        ag_copy(ph, g, 2, opp).wait_recv()
        ag_copy(ph, g, 3, opp).wait_recv()

    def chunk_rows(c):
        return pl.ds(pl.multiple_of(c * RC, RC), RC)

    def rs_copy(ph, c, kind):
        rows = chunk_rows(c)
        src, dst, where = (
            (part.at[ph, opp, rows, halves[0]], relay.at[ph, 0, rows], left),
            (part.at[ph, opp, rows, halves[1]], relay.at[ph, 1, rows], right),
            (part.at[ph, left, rows, halves[1]], frm.at[ph, 1, rows, halves[1]], left),
            (part.at[ph, right, rows, halves[0]], frm.at[ph, 0, rows, halves[0]], right),
            (part.at[ph, left, rows, halves[0]], frm.at[ph, 1, rows, halves[0]], left),
            (part.at[ph, right, rows, halves[1]], frm.at[ph, 0, rows, halves[1]], right),
        )[kind]
        return remote(src, dst, rs_ssem.at[ph, c, kind], rs_rsem.at[ph, c, kind], {"dp": where})

    def rs_start(ph, c, value):
        for j in range(4):
            part[ph, j, chunk_rows(c)] = value[:, j * Q : (j + 1) * Q].astype(BF16)
        for kind in range(4):
            rs_copy(ph, c, kind).start()

    def rs_relay(ph, c):
        rows = chunk_rows(c)
        for kind, target in ((0, left), (1, right)):
            rs_copy(ph, c, kind).wait_recv()
            own = part[ph, target, rows, halves[kind]].astype(F32)
            part[ph, target, rows, halves[kind]] = (own + relay[ph, kind, rows].astype(F32)).astype(BF16)
            rs_copy(ph, c, 4 + kind).start()

    def rs_finish(ph, c):
        for kind in (2, 3, 4, 5):
            rs_copy(ph, c, kind).wait_recv()

        @pl.loop(0, GC * G // 4)
        def _(sub):
            base = c * (GC * G) + sub * 4
            rows = pl.ds(pl.multiple_of(base * R, 4 * R), 4 * R)
            total = part[ph, x, rows].astype(F32) + frm[ph, 0, rows].astype(F32) + frm[ph, 1, rows].astype(F32)
            total = total.astype(BF16)
            stacked = jnp.concatenate([total[:, :W], total[:, W:]], axis=0)
            block = jnp.dot(perm[0], stacked, preferred_element_type=F32)
            leaving[ph, pl.ds(pl.multiple_of(base, 4), 4)] = block.reshape(4, R2, W).astype(BF16)

            @pl.loop(jnp.maximum(base, 1), base + 4)
            def _(k):
                remote(
                    leaving.at[ph, k],
                    returned.at[ph, k],
                    a2a_ssem.at[2 + ph],
                    a2a_rsem.at[2 + ph, lax.div(k, G)],
                    {"expert": lax.rem(me + n - k, n)},
                ).start()

    def fwd(c):
        rows = chunk_rows(c)
        block = jnp.concatenate([full[0, j, rows] for j in range(4)], axis=1)
        pre_gate = jnp.dot(block, gate_v[...], preferred_element_type=F32)
        pre_up = jnp.dot(block, up_v[...], preferred_element_type=F32)
        pg_v[rows, :] = pre_gate
        pu_v[rows, :] = pre_up
        hidden = (pre_gate * jax.nn.sigmoid(pre_gate) * pre_up).astype(BF16)
        hid_v[rows, :] = hidden
        return jnp.dot(hidden, down_v[...], preferred_element_type=F32)

    def bwd(c):
        rows = chunk_rows(c)
        block = jnp.concatenate([full[1, j, rows] for j in range(4)], axis=1)
        grad_hidden = lax.dot_general(block, down_v[...], LAST, preferred_element_type=F32)
        pre_gate = pg_v[rows, :]
        pre_up = pu_v[rows, :]
        s = jax.nn.sigmoid(pre_gate)
        grad_gate = (grad_hidden * pre_up * (s * (1.0 + pre_gate * (1.0 - s)))).astype(BF16)
        grad_up = (grad_hidden * (pre_gate * s)).astype(BF16)
        gpg_v[rows, :] = grad_gate
        gpu_v[rows, :] = grad_up
        value = lax.dot_general(grad_gate, gate_v[...], LAST, preferred_element_type=F32)
        return value + lax.dot_general(grad_up, up_v[...], LAST, preferred_element_type=F32)

    @pl.loop(0, NG)
    def _(g):
        ag_start(0, g)

        @pl.when(g > 0)
        def _():
            ag_forward(0, g - 1)

    ag_forward(0, NG - 1)
    for load in loads[4:]:
        load.wait()

    @pl.loop(0, NC)
    def _(c):
        for i in range(GC):
            g = c * GC + i
            ag_start(1, g)

            @pl.when(g > 0)
            def _():
                ag_forward(1, g - 1)

        for i in range(GC):
            ag_finish(0, c * GC + i)
        rs_start(0, c, fwd(c))

        @pl.when(c > 0)
        def _():
            rs_relay(0, c - 1)

    ag_forward(1, NG - 1)
    rs_relay(0, NC - 1)

    @pl.loop(0, NC)
    def _(c):
        for i in range(GC):
            ag_finish(1, c * GC + i)
        rs_start(1, c, bwd(c))
        rs_finish(0, c)

        @pl.when(c > 0)
        def _():
            rs_relay(1, c - 1)

    rs_relay(1, NC - 1)
    returned[0, 0] = leaving[0, 0]

    @pl.loop(0, NC)
    def _(c):
        rs_finish(1, c)

    returned[1, 0] = leaving[1, 0]

    def combine(ph, weights):
        total = jnp.zeros((2 * T, W), F32)

        def step(g, total):
            a2a_wait(2 + ph, returned.at[ph], g)
            ks = pl.ds(pl.multiple_of(g * G, G), G)
            rows = pl.ds(pl.multiple_of(g * G * R2, G * R2), G * R2)
            block = returned[ph, ks].astype(F32).reshape(G * R2, W).astype(BF16)
            for weight in weights:
                total = total + lax.dot_general(weight[rows, :], block, FIRST, preferred_element_type=F32)
            return total

        total = lax.fori_loop(0, NG, step, total)
        return jnp.concatenate([total[:T], total[T:]], axis=1).astype(BF16)

    def lanes_of(q):
        return pl.ds(pl.multiple_of(q * Q, Q), Q)

    def fin_copy(ph, ref, q, peer, slot):
        src = ref.at[:, lanes_of(q)]
        return remote(src, src, fin_ssem.at[ph, peer], fin_rsem.at[ph, slot], {"dp": peer})

    def fin_start(ph, ref, value):
        ref[:, lanes_of(x)] = value
        for peer in peers:
            fin_copy(ph, ref, x, peer, x).start()

    def fin_finish(ph, ref):
        for peer in peers:
            fin_copy(ph, ref, peer, peer, peer).wait_recv()

    stores = []

    def store(src, dst):
        copy = pltpu.make_async_copy(src, dst, store_sem.at[len(stores)])
        copy.start()
        stores.append(copy)

    fin_start(0, mixed_v, combine(0, (pph, ppl)))

    @pl.loop(0, 4)
    def _(j):
        rows = pl.ds(pl.multiple_of(j * Q, Q), Q)
        block = full[0, j]
        gg_v[rows, :] = (lax.dot_general(block, gpg_v[...], FIRST, preferred_element_type=F32) * scaling).astype(BF16)
        gu_v[rows, :] = (lax.dot_general(block, gpu_v[...], FIRST, preferred_element_type=F32) * scaling).astype(BF16)
        gd_v[:, rows] = (
            lax.dot_general(hid_v[...], full[1, j], FIRST, preferred_element_type=F32) * scaling
        ).astype(BF16)

    store(gg_v, gg_out.at[0])
    store(gu_v, gu_out.at[0])
    store(gd_v, gd_out.at[0])
    fin_start(1, glat_v, combine(1, (pp,)))
    fin_finish(0, mixed_v)
    store(mixed_v, mixed_out)
    lo_v[...] = jnp.dot(mixed_v[...], fl_v[...], preferred_element_type=F32).astype(BF16)
    store(lo_v, lo_out)
    fin_finish(1, glat_v)
    store(glat_v, glat_out)
    gt_v[...] = lax.dot_general(glat_v[...], tl_v[...], LAST, preferred_element_type=F32).astype(BF16)
    store(gt_v, gt_out)

    for ph in range(2):
        for peer in peers:
            xs_copy(ph, peer).wait_send()
        fin_ref = (mixed_v, glat_v)[ph]
        for peer in peers:
            fin_copy(ph, fin_ref, x, peer, x).wait_send()
        for buf, sem in ((outgoing.at[ph], a2a_ssem.at[ph]), (leaving.at[ph], a2a_ssem.at[2 + ph])):
            pltpu.make_async_copy(buf.at[1:n], buf.at[1:n], sem).wait()

        @pl.loop(0, NG)
        def _(g):
            for kind, q in ((0, x), (1, x), (2, left), (3, right)):
                ag_copy(ph, g, kind, q).wait_send()

        @pl.loop(0, NC)
        def _(c):
            for kind in range(6):
                rs_copy(ph, c, kind).wait_send()

    for copy in stores:
        copy.wait()


def layer_call(capacity, n, routes, slot_index, route_gates, tokens, to_latent, from_latent, gate, up, down, grad_output):
    T, Dd = tokens.shape
    L = to_latent.shape[1]
    Hs = gate.shape[2]
    Q, W = L // 4, L // 8
    R = capacity
    G = 8 if n >= 16 else 4
    NG = n // G
    NC = min(4, NG)
    cfg = dict(n=n, T=T, R=R, L=L, Q=Q, W=W, G=G, NG=NG, NC=NC, scaling=float((T * n) ** -0.5))
    rows = n * R
    vm = lambda shape, dtype=BF16: pltpu.VMEM(shape, dtype)
    dma = lambda *shape: pltpu.SemaphoreType.DMA(shape)
    any_spec = pl.BlockSpec(memory_space=pl.ANY)
    vm_spec = pl.BlockSpec(memory_space=pltpu.VMEM)
    outs = [
        ((T, Dd), BF16),
        ((T, Dd), BF16),
        (gate.shape, BF16),
        (up.shape, BF16),
        (down.shape, BF16),
        ((T, L), BF16),
        ((T, L), BF16),
    ]
    scratch = [
        vm((T, Dd)),
        vm((Dd, L)),
        vm((L, Dd)),
        vm((L, Hs)),
        vm((L, Hs)),
        vm((Hs, L)),
        vm((T, Dd)),
        vm((T, Dd)),
        vm((T, Dd)),
        vm((L, Hs)),
        vm((L, Hs)),
        vm((Hs, L)),
        vm((T, L)),
        vm((T, L)),
        vm((2, 4, T, Q)),
        vm((2, 4, T, Q)),
        vm((n, T), jnp.int32),
        vm((n, T), F32),
        vm((2 * rows, 2 * T)),
        vm((2 * rows, 2 * T)),
        vm((2 * rows, 2 * T)),
        vm((2, 8 * R, 8 * R)),
        vm((2, n, 2 * R, W)),
        vm((2, n, 2 * R, W)),
        vm((2, n, 2 * R, W)),
        vm((2, n, 2 * R, W)),
        vm((2, 4, rows, Q)),
        vm((2, 4, rows, Q)),
        vm((2, 2, rows, W)),
        vm((2, 2, rows, Q)),
        vm((rows, Hs), F32),
        vm((rows, Hs), F32),
        vm((rows, Hs)),
        vm((rows, Hs)),
        vm((rows, Hs)),
        dma(7),
        dma(7),
        dma(2, 4),
        dma(2, 4),
        dma(4),
        dma(4, NG),
        dma(2, NG, 4),
        dma(2, NG, 4),
        dma(2, NC, 6),
        dma(2, NC, 6),
        dma(2, 4),
        dma(2, 4),
    ]
    flops = 2 * rows * L * Hs * 9 + 2 * T * L * Dd * 4
    return pl.pallas_call(
        functools.partial(layer_kernel, cfg),
        out_shape=[jax.ShapeDtypeStruct(s, d) for s, d in outs],
        in_specs=[vm_spec] * 3 + [any_spec] * 7,
        out_specs=[any_spec] * len(outs),
        scratch_shapes=scratch,
        compiler_params=pltpu.CompilerParams(
            collective_id=0, has_side_effects=True, vmem_limit_bytes=62 * 1024 * 1024
        ),
        cost_estimate=pl.CostEstimate(flops=flops, bytes_accessed=16 * 2**20, transcendentals=rows * Hs),
    )(routes.T, slot_index.T, route_gates.T, tokens, to_latent, from_latent, gate, up, down, grad_output)


def spread_grad(left_side, right_side, scaling):
    return lax.psum_scatter(
        lax.dot_general(left_side, right_side, FIRST, preferred_element_type=F32) * scaling,
        "expert",
        scatter_dimension=0,
        tiled=True,
    )


def local(
    tokens,
    to_latent,
    from_latent,
    expert_gate,
    expert_up,
    expert_down,
    routes,
    slot_index,
    route_gates,
    grad_output,
):
    expert_count = lax.axis_size("expert")
    dp_count = lax.axis_size("dp")
    token_count, route_count = routes.shape
    capacity = dp_count * max(
        1,
        min(
            token_count // (4 * dp_count),
            5 * token_count * route_count // (4 * expert_count * dp_count),
        ),
    )
    scaling = (token_count * expert_count) ** (-0.5)
    layer_output, grad_tokens, grad_gate, grad_up, grad_down, mixed, grad_latent = layer_call(
        capacity,
        expert_count,
        routes,
        slot_index,
        route_gates,
        tokens,
        to_latent,
        from_latent,
        expert_gate,
        expert_up,
        expert_down,
        grad_output,
    )
    grad_from_latent = spread_grad(mixed, grad_output, scaling)
    grad_to_latent = spread_grad(grad_latent, tokens, scaling)
    return (
        layer_output,
        grad_tokens,
        grad_to_latent,
        grad_from_latent,
        grad_gate,
        grad_up,
        grad_down,
    )


def solution(mesh):
    return jax.shard_map(
        local,
        mesh=mesh,
        in_specs=(
            P("expert", "dp"),
            P("dp", None),
            P(None, "dp"),
            P("expert", None, "dp"),
            P("expert", None, "dp"),
            P("expert", "dp", None),
            P("expert", None),
            P("expert", None),
            P("expert", None),
            P("expert", "dp"),
        ),
        out_specs=(
            P("expert", "dp"),
            P("expert", "dp"),
            P("expert", "dp"),
            P("expert", "dp"),
            P("expert", None, "dp"),
            P("expert", None, "dp"),
            P("expert", "dp", None),
        ),
        check_vma=False,
    )
```

time: 790 us -> 450 us (0.57)
  waiting for transfers between devices: 590 us -> 279 us
  Pallas kernels: 0 us -> 140 us
  local copies, waits for them, and re-layouts: 85.7 us -> 5.31 us
  matrix products: 51.4 us -> 6.38 us
  starting transfers between devices: 33.7 us -> 0.08 us
  other arithmetic: 9.1 us -> 0 us
    all_to_all x4 -> x0, waiting for transfers between devices: 229 us -> none  [the longest x2 116 us: send_rows(): lax.all_to_all(row_block, 'expert', split_axis=0, concat_axis=0, tiled=True)]
    pallas_call x0 -> x1, Pallas kernels: none -> 140 us  [layer_call(): pl.pallas_call(functools.partial(layer_kernel, cfg), out_shape=[jax.Shape...]
    psum x2 -> x0, waiting for transfers between devices: 88 us -> none  [dp_total(): return lax.psum(summand.astype(jnp.bfloat16), 'dp').astype(jnp.float32)]
    dot_general x16 -> x2, matrix products: 51.4 us -> 6.38 us  [spread_grad(): lax.dot_general(left_side, right_side, FIRST, preferred_element_type=F32)]
    reshape x9 -> x0, local copies, waits for them, and re-layouts: 41.5 us -> none  [the longest x2 10.4 us: return_rows(): arrived.reshape(-1, latent_width)]
    all_to_all x4 -> x0, starting transfers between devices: 33.3 us -> none  [the longest x2 19.9 us: send_rows(): lax.all_to_all(row_block, 'expert', split_axis=0, concat_axis=0, tiled=True)]
    gather x4 -> x0, local copies, waits for them, and re-layouts: 30.7 us -> none  [the longest x2 17 us: return_rows(): return flat_rows[places]]
  transfers between devices with their start and end apart: 8 -> 2, of which waited for: 8 -> 2; matrix products, arithmetic and copies ran while one was open for 10% -> 1% of each run, Pallas kernels for 0% -> 0%
where the time goes in v1:
time: 450 us; the launch traced here: 445 us
  waiting for transfers between devices  279 us (62%)
  Pallas kernels  140 us (31%)
  between operations  14.1 us (3%)
  matrix products  6.38 us (1%)
  local copies, waits for them, and re-layouts  5.31 us (1%)
    reduce_scatter x2, waiting for transfers between devices, spread_grad(): lax.psum_scatter(lax.dot_general(left_side, right_side, FIRST, preferred_...  279 us
    pallas_call x1, Pallas kernels, layer_call(): pl.pallas_call(functools.partial(layer_kernel, cfg), out_shape=[jax.Shape...  140 us
  transfers between devices with their start and end apart: 2, of which 2 were waited for; matrix products, arithmetic and copies ran while one was open for 1% of the time, Pallas kernels for 0%

profile of v1, /device:TPU:1, one launch (start us, length us, event | category | flops | bytes accessed | tf_op | source)
XLA Modules:
  0.0 445.4 jit_solution(1929384864894055154)
XLA Ops:
  7.2 0.0 reduce-scatter.3.cloned.1.call-start
  7.2 0.0 copy-start.3
  7.2 140.2 %shard_map.153 = (bf16[128,1024]{1,0:T(8,128)(2,1)}, bf16[128,1024]{1,0:T(8,128)(2,1)}, bf16[1,1024,512]{2,1,0:T(8,128)(2,1)}, bf16[1,1024,512]{2,1,0:T(8,128)(2...) custom-call(s32[8,128]{1,0:T(8,128)} %bitcast.7, s32[8,128]{1,0:T(8,128)} %bitcast.8, ...), custom_call_target="tpu_custom_call" | custom-call | flops 13153337344 | bytes 16777216 | tf_op jit(solution)/shard_map/pallas_call | solution.py:561
  147.4 0.0 copy-done.3
  147.5 0.0 copy-start.4
  147.5 0.0 copy-start.5
  147.5 3.7 convolution_multiply_fusion.1
  151.1 0.0 reduce-scatter.3.cloned.1.call-update
  151.2 0.0 reduce-scatter.5.cloned.1.call-start
  151.2 0.0 copy-done.4
  151.2 0.0 copy-done.5
  151.2 0.0 copy-start.6
  151.2 0.0 copy-start.2
  151.3 2.7 convolution_multiply_fusion
  154.0 0.0 copy-start.1
  154.0 0.0 copy-start
  154.0 0.0 reduce-scatter.5.cloned.1.call-update
  154.0 131.9 %reduce-scatter.3.cloned.1.call-done = f32[16,1024]{1,0:T(8,128)} async-done(((f32[1024,1024]{1,0:T(8,128)}), f32[16,1024]{1,0:T(8,128)}) %reduce-scatter.3.cloned.1.call-update) | async-done | bytes 65552 | tf_op jit(solution)/shard_map/reduce_scatter | solution.py:575
  285.9 147.4 %reduce-scatter.5.cloned.1.call-done = f32[16,1024]{1,0:T(8,128)} async-done(((f32[1024,1024]{1,0:T(8,128)}), f32[16,1024]{1,0:T(8,128)}) %reduce-scatter.5.cloned.1.call-update) | async-done | bytes 65552 | tf_op jit(solution)/shard_map/reduce_scatter | solution.py:575
  433.3 1.7 copy.22
  434.9 0.0 copy-done.6
  434.9 0.7 copy.23
  435.6 0.0 copy-done.2
  435.6 1.0 copy.24
  436.6 0.0 copy-done.1
  436.6 1.0 copy.25
  437.6 0.0 copy-done
  437.6 1.0 copy.26
Async XLA Ops:
  7.2 278.7 %reduce-scatter.3.cloned.1.call-start = ((), (), s32[]{:S(2)}) async-start(), calls=%async_computation.2 | async-start | bytes 4259840 | tf_op jit(solution)/shard_map/reduce_scatter | solution.py:575
  7.2 140.2 %copy-start.3 = (bf16[128,1024]{1,0:T(8,128)(2,1)S(1)}, bf16[128,1024]{1,0:T(8,128)(2,1)}, u32[]{:S(2)}) copy-start(bf16[128,1024]{1,0:T(8,128)(2,1)} %tok_in.1) | copy-start | bytes 786436
  147.5 3.8 copy-start.4
  147.5 3.8 copy-start.5
  151.2 282.1 %reduce-scatter.5.cloned.1.call-start = ((), (), s32[]{:S(2)}) async-start(), calls=%async_computation.3 | async-start | bytes 4259840 | tf_op jit(solution)/shard_map/reduce_scatter | solution.py:575
  151.2 283.7 %copy-start.6 = (bf16[128,1024]{1,0:T(8,128)(2,1)S(1)}, bf16[128,1024]{1,0:T(8,128)(2,1)}, u32[]{:S(2)}) copy-start(bf16[128,1024]{1,0:T(8,128)(2,1)} %get-tuple-element.29) | copy-start | bytes 786436
  151.2 284.4 %copy-start.2 = (bf16[1,1024,512]{2,1,0:T(8,128)(2,1)S(1)}, bf16[1,1024,512]{2,1,0:T(8,128)(2,1)}, u32[]{:S(2)}) copy-start(bf16[1,1024,512]{2,1,0:T(8,128)(2,1)} %get-tuple-element.32) | copy-start | bytes 3145732
  154.0 282.6 %copy-start.1 = (bf16[1,1024,512]{2,1,0:T(8,128)(2,1)S(1)}, bf16[1,1024,512]{2,1,0:T(8,128)(2,1)}, u32[]{:S(2)}) copy-start(bf16[1,1024,512]{2,1,0:T(8,128)(2,1)} %get-tuple-element.33) | copy-start | bytes 3145732
  154.0 283.6 %copy-start = (bf16[1,512,1024]{2,1,0:T(8,128)(2,1)S(1)}, bf16[1,512,1024]{2,1,0:T(8,128)(2,1)}, u32[]{:S(2)}) copy-start(bf16[1,512,1024]{2,1,0:T(8,128)(2,1)} %get-tuple-element.34) | copy-start | bytes 3145732
Sparse Core Ops, SparseCore 0:
  151.3 134.5 reduce-scatter.2
  291.1 142.0 reduce-scatter.4

commit v2 on v1

--- a/solution.py
+++ b/solution.py
@@ -37,8 +37,8 @@
     gg_out,
     gu_out,
     gd_out,
-    mixed_out,
-    glat_out,
+    gtl_out,
+    gfl_out,
     tok_v,
     tl_v,
     fl_v,
@@ -51,8 +51,14 @@
     gg_v,
     gu_v,
     gd_v,
-    mixed_v,
-    glat_v,
+    lat_v,
+    sel_v,
+    gpart,
+    grelay,
+    gfrm,
+    zsend,
+    zrecv,
+    gsum,
     xs_send_v,
     xs_recv_v,
     s_tab,
@@ -86,7 +92,14 @@
     rs_rsem,
     fin_ssem,
     fin_rsem,
+    sib_ssem,
+    sib_rsem,
+    ring_ssem,
+    ring_rsem,
+    z_ssem,
+    z_rsem,
 ):
+    Z, RB, Dd = cfg["Z"], cfg["RB"], cfg["Dd"]
     n, T, R, L, Q, W, G, NG, NC = (cfg[k] for k in ("n", "T", "R", "L", "Q", "W", "G", "NG", "NC"))
     scaling = cfg["scaling"]
     R2 = 2 * R
@@ -99,14 +112,25 @@
     left = lax.rem(x + 3, 4)
     opp = lax.rem(x + 2, 4)
     peers = (right, left, opp)
+    core = lax.rem(me, 2)
+    y = lax.rem(lax.div(me, 2), 4)
+    z = lax.div(me, 8)
+    sibling = {"expert": me + 1 - 2 * core}
+
+    def at_y(other):
+        return {"expert": (z * 4 + other) * 2 + core}
+
+    y_right = lax.rem(y + 1, 4)
+    y_left = lax.rem(y + 3, 4)
+    y_opp = lax.rem(y + 2, 4)
 
     loads = [
         pltpu.make_async_copy(src, dst, load_sem.at[i])
         for i, (src, dst) in enumerate(
             (
-                (tok_in, tok_v),
+                (tok_in, tok_v.at[core]),
                 (tl_in, tl_v),
-                (go_in, go_v),
+                (go_in, go_v.at[core]),
                 (fl_in, fl_v),
                 (gate_in.at[0], gate_v),
                 (up_in.at[0], up_v),
@@ -170,14 +194,27 @@
         total = total.astype(BF16)
         return jnp.concatenate([total[:, :W], total[:, W:]], axis=0)
 
+    def sib_copy(i):
+        ref = (tok_v, go_v)[i].at[core]
+        return remote(ref, ref, sib_ssem.at[i], sib_rsem.at[i], sibling)
+
     loads[0].wait()
     loads[1].wait()
-    latent_part = jnp.dot(tok_v[...], tl_v[...], preferred_element_type=F32)
+    latent_part = jnp.dot(tok_v[core], tl_v[...], preferred_element_type=F32)
     pl.semaphore_wait(barrier, n - 1 + 3)
     xs_start(0, latent_part)
     loads[2].wait()
     loads[3].wait()
-    xs_start(1, lax.dot_general(go_v[...], fl_v[...], LAST, preferred_element_type=F32))
+    xs_start(1, lax.dot_general(go_v[core], fl_v[...], LAST, preferred_element_type=F32))
+    sib_copy(0).start()
+    sib_copy(1).start()
+
+    srow = lax.broadcasted_iota(jnp.int32, (1, L // 2), 1)
+    sy = lax.shift_right_logical(srow, (Z * RB).bit_length() - 1)
+    sz = lax.shift_right_logical(srow, RB.bit_length() - 1) & (Z - 1)
+    want = ((sz * 4 + sy) * 2 + core) * RB + (srow & (RB - 1))
+    scol = lax.broadcasted_iota(jnp.int32, (L, L // 2), 0)
+    sel_v[...] = jnp.where(scol == want, 1.0, 0.0).astype(BF16)
 
     r_iota = lax.broadcasted_iota(jnp.int32, (G, R2, T), 1)
 
@@ -416,18 +453,100 @@
     def lanes_of(q):
         return pl.ds(pl.multiple_of(q * Q, Q), Q)
 
-    def fin_copy(ph, ref, q, peer, slot):
-        src = ref.at[:, lanes_of(q)]
+    def fin_copy(ph, q, peer, slot):
+        src = lat_v.at[ph, core, :, lanes_of(q)]
         return remote(src, src, fin_ssem.at[ph, peer], fin_rsem.at[ph, slot], {"dp": peer})
 
-    def fin_start(ph, ref, value):
-        ref[:, lanes_of(x)] = value
+    def fin_sib(ph, q, whose):
+        src = lat_v.at[ph, whose, :, lanes_of(q)]
+        return remote(src, src, sib_ssem.at[2 + 4 * ph + q], sib_rsem.at[2 + 4 * ph + q], sibling)
+
+    def fin_start(ph, value):
+        lat_v[ph, core, :, lanes_of(x)] = value
         for peer in peers:
-            fin_copy(ph, ref, x, peer, x).start()
-
-    def fin_finish(ph, ref):
+            fin_copy(ph, x, peer, x).start()
+        fin_sib(ph, x, core).start()
+
+    def fin_finish(ph):
         for peer in peers:
-            fin_copy(ph, ref, peer, peer, peer).wait_recv()
+            fin_copy(ph, peer, peer, peer).wait_recv()
+            fin_sib(ph, peer, core).start()
+
+    cols = Dd // 2
+
+    def col_chunk(c):
+        return slice(c * cols, (c + 1) * cols)
+
+    def ring_copy(ph, c, kind):
+        base = c * cols
+        parts = (slice(base, base + cols // 2), slice(base + cols // 2, base + cols))
+        src, dst, where = (
+            (gpart.at[ph, y_opp, :, parts[0]], grelay.at[ph, c, 0], y_left),
+            (gpart.at[ph, y_opp, :, parts[1]], grelay.at[ph, c, 1], y_right),
+            (gpart.at[ph, y_left, :, parts[1]], gfrm.at[ph, 1, :, parts[1]], y_left),
+            (gpart.at[ph, y_right, :, parts[0]], gfrm.at[ph, 0, :, parts[0]], y_right),
+            (gpart.at[ph, y_left, :, parts[0]], gfrm.at[ph, 1, :, parts[0]], y_left),
+            (gpart.at[ph, y_right, :, parts[1]], gfrm.at[ph, 0, :, parts[1]], y_right),
+        )[kind]
+        return remote(src, dst, ring_ssem.at[ph, c, kind], ring_rsem.at[ph, c, kind], at_y(where))
+
+    def ring_start(ph):
+        if ph == 0:
+            sib_copy(1).wait_recv()
+        else:
+            sib_copy(0).wait_recv()
+        for q in range(4):
+            fin_sib(ph, q, 1 - core).wait_recv()
+        other = (go_v, tok_v)[ph]
+        chosen = jnp.dot(lat_v[ph].reshape(2 * T, L), sel_v[...], preferred_element_type=F32).astype(BF16)
+        for c in range(2):
+            right_side = other[:, :, col_chunk(c)].reshape(2 * T, cols)
+            value = lax.dot_general(chosen, right_side, FIRST, preferred_element_type=F32).astype(BF16)
+            gpart[ph, :, :, col_chunk(c)] = value.reshape(4, Z * RB, cols)
+            for kind in range(4):
+                ring_copy(ph, c, kind).start()
+
+    def ring_relay(ph):
+        for c in range(2):
+            base = c * cols
+            parts = (slice(base, base + cols // 2), slice(base + cols // 2, base + cols))
+            for kind, target in ((0, y_left), (1, y_right)):
+                ring_copy(ph, c, kind).wait_recv()
+                own = gpart[ph, target, :, parts[kind]].astype(F32)
+                gpart[ph, target, :, parts[kind]] = (own + grelay[ph, c, kind].astype(F32)).astype(BF16)
+                ring_copy(ph, c, 4 + kind).start()
+
+    def z_copy(ph, c, step, source, target):
+        return remote(
+            zsend.at[ph, target, :, col_chunk(c)],
+            zrecv.at[ph, source, :, col_chunk(c)],
+            z_ssem.at[ph, c, step],
+            z_rsem.at[ph, c, step],
+            {"expert": (target * 4 + y) * 2 + core},
+        )
+
+    def ring_finish(ph):
+        for c in range(2):
+            for kind in (2, 3, 4, 5):
+                ring_copy(ph, c, kind).wait_recv()
+            here = col_chunk(c)
+            total = gpart[ph, y, :, here].astype(F32) + gfrm[ph, 0, :, here].astype(F32) + gfrm[ph, 1, :, here].astype(F32)
+            total = total.reshape(Z, RB, cols)
+            gsum[ph, :, :, here] = total
+            zsend[ph, :, :, here] = total.astype(BF16)
+            for step in range(1, Z):
+                z_copy(ph, c, step, z, lax.rem(z + step, Z)).start()
+
+    def z_finish(ph):
+        for c in range(2):
+            here = col_chunk(c)
+            total = gsum[ph, z, :, here]
+            for step in range(1, Z):
+                source = lax.rem(z + Z - step, Z)
+                z_copy(ph, c, step, source, z).wait_recv()
+                total = total + zrecv[ph, source, :, here].astype(F32)
+            gsum[ph, z, :, here] = total * scaling
+        store(gsum.at[ph, z], (gfl_out, gtl_out)[ph])
 
     stores = []
 
@@ -436,7 +555,7 @@
         copy.start()
         stores.append(copy)
 
-    fin_start(0, mixed_v, combine(0, (pph, ppl)))
+    fin_start(0, combine(0, (pph, ppl)))
 
     @pl.loop(0, 4)
     def _(j):
@@ -444,29 +563,47 @@
         block = full[0, j]
         gg_v[rows, :] = (lax.dot_general(block, gpg_v[...], FIRST, preferred_element_type=F32) * scaling).astype(BF16)
         gu_v[rows, :] = (lax.dot_general(block, gpu_v[...], FIRST, preferred_element_type=F32) * scaling).astype(BF16)
+
+    store(gg_v, gg_out.at[0])
+    store(gu_v, gu_out.at[0])
+    fin_finish(0)
+    lo_v[...] = jnp.dot(lat_v[0, core], fl_v[...], preferred_element_type=F32).astype(BF16)
+    store(lo_v, lo_out)
+    ring_start(0)
+
+    @pl.loop(0, 4)
+    def _(j):
+        rows = pl.ds(pl.multiple_of(j * Q, Q), Q)
         gd_v[:, rows] = (
             lax.dot_general(hid_v[...], full[1, j], FIRST, preferred_element_type=F32) * scaling
         ).astype(BF16)
 
-    store(gg_v, gg_out.at[0])
-    store(gu_v, gu_out.at[0])
     store(gd_v, gd_out.at[0])
-    fin_start(1, glat_v, combine(1, (pp,)))
-    fin_finish(0, mixed_v)
-    store(mixed_v, mixed_out)
-    lo_v[...] = jnp.dot(mixed_v[...], fl_v[...], preferred_element_type=F32).astype(BF16)
-    store(lo_v, lo_out)
-    fin_finish(1, glat_v)
-    store(glat_v, glat_out)
-    gt_v[...] = lax.dot_general(glat_v[...], tl_v[...], LAST, preferred_element_type=F32).astype(BF16)
+    ring_relay(0)
+    fin_start(1, combine(1, (pp,)))
+    ring_finish(0)
+    fin_finish(1)
+    gt_v[...] = lax.dot_general(lat_v[1, core], tl_v[...], LAST, preferred_element_type=F32).astype(BF16)
     store(gt_v, gt_out)
+    ring_start(1)
+    z_finish(0)
+    ring_relay(1)
+    ring_finish(1)
+    z_finish(1)
 
     for ph in range(2):
         for peer in peers:
             xs_copy(ph, peer).wait_send()
-        fin_ref = (mixed_v, glat_v)[ph]
+        sib_copy(ph).wait_send()
         for peer in peers:
-            fin_copy(ph, fin_ref, x, peer, x).wait_send()
+            fin_copy(ph, x, peer, x).wait_send()
+        for q in range(4):
+            fin_sib(ph, q, core).wait_send()
+        for c in range(2):
+            for kind in range(6):
+                ring_copy(ph, c, kind).wait_send()
+            for step in range(1, Z):
+                z_copy(ph, c, step, z, lax.rem(z + step, Z)).wait_send()
         for buf, sem in ((outgoing.at[ph], a2a_ssem.at[ph]), (leaving.at[ph], a2a_ssem.at[2 + ph])):
             pltpu.make_async_copy(buf.at[1:n], buf.at[1:n], sem).wait()
 
@@ -493,7 +630,8 @@
     G = 8 if n >= 16 else 4
     NG = n // G
     NC = min(4, NG)
-    cfg = dict(n=n, T=T, R=R, L=L, Q=Q, W=W, G=G, NG=NG, NC=NC, scaling=float((T * n) ** -0.5))
+    Z, RB = n // 8, L // n
+    cfg = dict(Z=Z, RB=RB, Dd=Dd, n=n, T=T, R=R, L=L, Q=Q, W=W, G=G, NG=NG, NC=NC, scaling=float((T * n) ** -0.5))
     rows = n * R
     vm = lambda shape, dtype=BF16: pltpu.VMEM(shape, dtype)
     dma = lambda *shape: pltpu.SemaphoreType.DMA(shape)
@@ -505,24 +643,30 @@
         (gate.shape, BF16),
         (up.shape, BF16),
         (down.shape, BF16),
-        ((T, L), BF16),
-        ((T, L), BF16),
+        ((RB, Dd), F32),
+        ((RB, Dd), F32),
     ]
     scratch = [
-        vm((T, Dd)),
+        vm((2, T, Dd)),
         vm((Dd, L)),
         vm((L, Dd)),
         vm((L, Hs)),
         vm((L, Hs)),
         vm((Hs, L)),
-        vm((T, Dd)),
+        vm((2, T, Dd)),
         vm((T, Dd)),
         vm((T, Dd)),
         vm((L, Hs)),
         vm((L, Hs)),
         vm((Hs, L)),
-        vm((T, L)),
-        vm((T, L)),
+        vm((2, 2, T, L)),
+        vm((L, L // 2)),
+        vm((2, 4, Z * RB, Dd)),
+        vm((2, 2, 2, Z * RB, Dd // 4)),
+        vm((2, 2, Z * RB, Dd)),
+        vm((2, Z, RB, Dd)),
+        vm((2, Z, RB, Dd)),
+        vm((2, Z, RB, Dd), F32),
         vm((2, 4, T, Q)),
         vm((2, 4, T, Q)),
         vm((n, T), jnp.int32),
@@ -556,6 +700,12 @@
         dma(2, NC, 6),
         dma(2, 4),
         dma(2, 4),
+        dma(10),
+        dma(10),
+        dma(2, 2, 6),
+        dma(2, 2, 6),
+        dma(2, 2, Z),
+        dma(2, 2, Z),
     ]
     flops = 2 * rows * L * Hs * 9 + 2 * T * L * Dd * 4
     return pl.pallas_call(
@@ -569,15 +719,6 @@
         ),
         cost_estimate=pl.CostEstimate(flops=flops, bytes_accessed=16 * 2**20, transcendentals=rows * Hs),
     )(routes.T, slot_index.T, route_gates.T, tokens, to_latent, from_latent, gate, up, down, grad_output)
-
-
-def spread_grad(left_side, right_side, scaling):
-    return lax.psum_scatter(
-        lax.dot_general(left_side, right_side, FIRST, preferred_element_type=F32) * scaling,
-        "expert",
-        scatter_dimension=0,
-        tiled=True,
-    )
 
 
 def local(
@@ -602,8 +743,7 @@
             5 * token_count * route_count // (4 * expert_count * dp_count),
         ),
     )
-    scaling = (token_count * expert_count) ** (-0.5)
-    layer_output, grad_tokens, grad_gate, grad_up, grad_down, mixed, grad_latent = layer_call(
+    (layer_output, grad_tokens, grad_gate, grad_up, grad_down, grad_to_latent, grad_from_latent) = layer_call(
         capacity,
         expert_count,
         routes,
@@ -617,8 +757,6 @@
         expert_down,
         grad_output,
     )
-    grad_from_latent = spread_grad(mixed, grad_output, scaling)
-    grad_to_latent = spread_grad(grad_latent, tokens, scaling)
     return (
         layer_output,
         grad_tokens,

time: 450 us -> 180 us (0.40)
  waiting for transfers between devices: 279 us -> 0 us
  Pallas kernels: 140 us -> 168 us
  between operations: 14.1 us -> 0.66 us
  matrix products: 6.38 us -> 0 us
  local copies, waits for them, and re-layouts: 5.31 us -> 10.7 us
    reduce_scatter x2 -> x0, waiting for transfers between devices: 279 us -> none  [spread_grad(): lax.psum_scatter(lax.dot_general(left_side, right_side, FIRST, preferred_...]
    pallas_call x1, Pallas kernels: 140 us -> 168 us  [layer_call(): pl.pallas_call(functools.partial(layer_kernel, cfg), out_shape=[jax.Shape...]
    dot_general x2 -> x0, matrix products: 6.38 us -> none  [spread_grad(): lax.dot_general(left_side, right_side, FIRST, preferred_element_type=F32)]
    unnamed x19 -> x11, local copies, waits for them, and re-layouts: 5.31 us -> 10.7 us
  transfers between devices with their start and end apart: 2 -> 0, of which waited for: 2 -> 0; matrix products, arithmetic and copies ran while one was open for 1% -> 0% of each run, Pallas kernels for 0% -> 0%
where the time goes in v2:
time: 180 us; the launch traced here: 179 us
  Pallas kernels  168 us (93%)
  local copies, waits for them, and re-layouts  10.7 us (6%)
    pallas_call x1, Pallas kernels, layer_call(): pl.pallas_call(functools.partial(layer_kernel, cfg), out_shape=[jax.Shape...  168 us
    unnamed x11, local copies, waits for them, and re-layouts  10.7 us

profile of v2, /device:TPU:1, one launch (start us, length us, event | category | flops | bytes accessed | tf_op | source)
XLA Modules:
  0.0 179.4 jit_solution(11529747848359961723)
XLA Ops:
  0.6 168.1 %shard_map.153 = (bf16[128,1024]{1,0:T(8,128)(2,1)}, bf16[128,1024]{1,0:T(8,128)(2,1)}, bf16[1,1024,512]{2,1,0:T(8,128)(2,1)}, bf16[1,1024,512]{2,1,0:T(8,128)(2...) custom-call(s32[8,128]{1,0:T(8,128)} %bitcast.3, s32[8,128]{1,0:T(8,128)} %bitcast.4, ...), custom_call_target="tpu_custom_call" | custom-call | flops 13153337344 | bytes 16777216 | tf_op jit(solution)/shard_map/pallas_call | solution.py:711
  168.7 0.0 copy-start.1
  168.7 1.8 copy.24
  170.5 1.7 copy.25
  172.1 1.5 copy.26
  173.6 1.5 copy.27
  175.1 0.0 copy-start
  175.1 2.4 %copy.28 = bf16[1,1024,512]{2,1,0:T(8,128)(2,1)} copy(bf16[1,1024,512]{2,1,0:T(8,128)(2,1)} %get-tuple-element.32) | data formatting | bytes 2097152
  177.4 0.0 copy-done.1
  177.4 1.0 copy.29
  178.4 0.0 copy-done
  178.4 1.0 copy.30
Async XLA Ops:
  168.7 8.7 %copy-start.1 = (bf16[1,1024,512]{2,1,0:T(8,128)(2,1)S(1)}, bf16[1,1024,512]{2,1,0:T(8,128)(2,1)}, u32[]{:S(2)}) copy-start(bf16[1,1024,512]{2,1,0:T(8,128)(2,1)} %get-tuple-element.33) | copy-start | bytes 3145732
  175.1 3.3 %copy-start = (bf16[1,512,1024]{2,1,0:T(8,128)(2,1)S(1)}, bf16[1,512,1024]{2,1,0:T(8,128)(2,1)}, u32[]{:S(2)}) copy-start(bf16[1,512,1024]{2,1,0:T(8,128)(2,1)} %get-tuple-element.34) | copy-start | bytes 3145732

commit v3 on v1

--- a/solution.py
+++ b/solution.py
@@ -37,22 +37,26 @@
     gg_out,
     gu_out,
     gd_out,
-    mixed_out,
-    glat_out,
-    tok_v,
+    gtl_out,
+    gfl_out,
+    tok_g,
     tl_v,
     fl_v,
     gate_v,
     up_v,
     down_v,
-    go_v,
+    go_g,
     lo_v,
     gt_v,
     gg_v,
     gu_v,
     gd_v,
-    mixed_v,
-    glat_v,
+    lat_v,
+    turned,
+    taken,
+    zsend,
+    zrecv,
+    gsum,
     xs_send_v,
     xs_recv_v,
     s_tab,
@@ -86,7 +90,19 @@
     rs_rsem,
     fin_ssem,
     fin_rsem,
+    sib_ssem,
+    sib_rsem,
+    near_ssem,
+    near_rsem,
+    turn_ssem,
+    turn_rsem,
+    z_ssem,
+    z_rsem,
+    y_ready,
+    core_ready,
 ):
+    Z, Y, RB, Dd = cfg["Z"], cfg["Y"], cfg["RB"], cfg["Dd"]
+    U = 2 * Y
     n, T, R, L, Q, W, G, NG, NC = (cfg[k] for k in ("n", "T", "R", "L", "Q", "W", "G", "NG", "NC"))
     scaling = cfg["scaling"]
     R2 = 2 * R
@@ -99,14 +115,38 @@
     left = lax.rem(x + 3, 4)
     opp = lax.rem(x + 2, 4)
     peers = (right, left, opp)
+    core = lax.rem(me, 2)
+    y = lax.rem(lax.div(me, 2), Y)
+    z = lax.div(me, 2 * Y)
+    unit = y * 2 + core
+
+    def at(zz, yy, cc):
+        return (zz * Y + yy) * 2 + cc
+
+    sibling = {"expert": at(z, y, 1 - core)}
+
+    def offsets(i):
+        j = i & (Z - 1)
+        u = lax.shift_right_logical(i, Z.bit_length() - 1)
+        step = lax.shift_right_logical(j + 1, 1)
+        dz = jnp.where((j & 1) == 1, step, Z - step)
+        return dz, lax.shift_right_logical(u, 1), u & 1
+
+    def target_of(i):
+        dz, dy, dc = offsets(i)
+        return at((z + dz) & (Z - 1), (y + dy) & (Y - 1), (core + dc) & 1)
+
+    def source_of(i):
+        dz, dy, dc = offsets(i)
+        return at((z + 2 * Z - dz) & (Z - 1), (y + Y - dy) & (Y - 1), (core + dc) & 1)
 
     loads = [
         pltpu.make_async_copy(src, dst, load_sem.at[i])
         for i, (src, dst) in enumerate(
             (
-                (tok_in, tok_v),
+                (tok_in, tok_g.at[0]),
                 (tl_in, tl_v),
-                (go_in, go_v),
+                (go_in, go_g.at[0]),
                 (fl_in, fl_v),
                 (gate_in.at[0], gate_v),
                 (up_in.at[0], up_v),
@@ -114,24 +154,28 @@
             )
         )
     ]
-    for load in loads:
+    for load in loads[:2]:
         load.start()
+
+    def signal(sem, where):
+        pl.semaphore_signal(sem, inc=1, device_id=where, device_id_type=MESH)
+
     barrier = pltpu.get_barrier_semaphore()
     for peer in peers:
-        pl.semaphore_signal(barrier, inc=1, device_id={"dp": peer}, device_id_type=MESH)
-
-    @pl.loop(1, n)
-    def _(k):
-        pl.semaphore_signal(barrier, inc=1, device_id={"expert": lax.rem(me + k, n)}, device_id_type=MESH)
-
-    krel = lax.broadcasted_iota(jnp.int32, (n, T), 0)
+        signal(barrier, {"dp": peer})
+    signal(barrier, sibling)
+    for step in range(1, Y):
+        signal(barrier, {"expert": at(z, (y + step) & (Y - 1), core)})
+    for step in range(1, Z):
+        signal(barrier, {"expert": at((z + step) & (Z - 1), y, core)})
+    near_count = 3 + 1 + (Y - 1) + (Z - 1)
+
+    whose = target_of(lax.broadcasted_iota(jnp.int32, (n, T), 0))
     s_val = jnp.full((n, T), -1000, jnp.int32)
     g_val = jnp.zeros((n, T), F32)
     for j in range(routes_ref.shape[0]):
-        rel = routes_ref[j : j + 1, :] - me
-        rel = jnp.where(rel < 0, rel + n, rel)
         slot = slots_ref[j : j + 1, :]
-        match = (krel == rel) & (slot < R)
+        match = (whose == routes_ref[j : j + 1, :]) & (slot < R)
         s_val = jnp.where(match, slot, s_val)
         g_val = jnp.where(match, gates_ref[j : j + 1, :], g_val)
     s_tab[...] = s_val
@@ -172,12 +216,21 @@
 
     loads[0].wait()
     loads[1].wait()
-    latent_part = jnp.dot(tok_v[...], tl_v[...], preferred_element_type=F32)
-    pl.semaphore_wait(barrier, n - 1 + 3)
+    loads[2].start()
+    loads[3].start()
+    latent_part = jnp.dot(tok_g[0], tl_v[...], preferred_element_type=F32)
+    pl.semaphore_wait(barrier, near_count)
     xs_start(0, latent_part)
+    for step in range(1, Y):
+        signal(y_ready, {"expert": at(z, (y + step) & (Y - 1), core)})
     loads[2].wait()
     loads[3].wait()
-    xs_start(1, lax.dot_general(go_v[...], fl_v[...], LAST, preferred_element_type=F32))
+    for load in loads[4:]:
+        load.start()
+    xs_start(1, lax.dot_general(go_g[0], fl_v[...], LAST, preferred_element_type=F32))
+    if Y > 1:
+        pl.semaphore_wait(y_ready, Y - 1)
+    signal(core_ready, sibling)
 
     r_iota = lax.broadcasted_iota(jnp.int32, (G, R2, T), 1)
 
@@ -215,13 +268,52 @@
                     arrived.at[ph, k],
                     a2a_ssem.at[ph],
                     a2a_rsem.at[ph, g],
-                    {"expert": lax.rem(me + k, n)},
+                    {"expert": target_of(k)},
                 ).start()
 
         arrived[ph, 0] = outgoing[ph, 0]
 
-    dispatch(0, xs_finish(0))
+    latent_rows = xs_finish(0)
+    pl.semaphore_wait(core_ready, 1)
+    dispatch(0, latent_rows)
     dispatch(1, xs_finish(1))
+
+    def sib_copy(i, dy):
+        ref = (tok_g, go_g)[i]
+        dst = ref.at[(2 * dy + 1 - 2 * core + U) & (U - 1)]
+        return remote(ref.at[2 * dy], dst, sib_ssem.at[i, dy], sib_rsem.at[i, dy], sibling)
+
+    def sib_wait(i, dy):
+        ref = (tok_g, go_g)[i]
+        here = (2 * dy + 2 * core - 1 + U) & (U - 1)
+        remote(ref.at[2 * dy], ref.at[here], sib_ssem.at[i, dy], sib_rsem.at[i, dy], sibling).wait_recv()
+
+    def near_copy(i, dy):
+        ref = (tok_g, go_g)[i]
+        return remote(
+            ref.at[0],
+            ref.at[2 * dy],
+            near_ssem.at[i, dy],
+            near_rsem.at[i, dy],
+            {"expert": at(z, (y + dy) & (Y - 1), core)},
+        )
+
+    def near_start(i):
+        sib_copy(i, 0).start()
+        for dy in range(1, Y):
+            near_copy(i, dy).start()
+
+    def near_forward(i):
+        for dy in range(1, Y):
+            near_copy(i, dy).wait_recv()
+            sib_copy(i, dy).start()
+
+    def near_finish(i):
+        for dy in range(Y):
+            sib_wait(i, dy)
+
+    near_start(1)
+    near_start(0)
 
     def a2a_wait(ph, buf, g):
         @pl.when(g == 0)
@@ -317,7 +409,7 @@
                     returned.at[ph, k],
                     a2a_ssem.at[2 + ph],
                     a2a_rsem.at[2 + ph, lax.div(k, G)],
-                    {"expert": lax.rem(me + n - k, n)},
+                    {"expert": source_of(k)},
                 ).start()
 
     def fwd(c):
@@ -399,35 +491,90 @@
     returned[1, 0] = leaving[1, 0]
 
     def combine(ph, weights):
-        total = jnp.zeros((2 * T, W), F32)
-
         def step(g, total):
             a2a_wait(2 + ph, returned.at[ph], g)
             ks = pl.ds(pl.multiple_of(g * G, G), G)
             rows = pl.ds(pl.multiple_of(g * G * R2, G * R2), G * R2)
             block = returned[ph, ks].astype(F32).reshape(G * R2, W).astype(BF16)
             for weight in weights:
-                total = total + lax.dot_general(weight[rows, :], block, FIRST, preferred_element_type=F32)
+                total = total + lax.dot_general(block, weight[rows, :], FIRST, preferred_element_type=F32)
             return total
 
-        total = lax.fori_loop(0, NG, step, total)
-        return jnp.concatenate([total[:T], total[T:]], axis=1).astype(BF16)
+        total = lax.fori_loop(0, NG, step, jnp.zeros((W, 2 * T), F32))
+        for h in range(2):
+            turned[ph, :, h] = total[:, h * T : (h + 1) * T].reshape(U, RB, T).astype(BF16)
+        taken[ph, 0] = turned[ph, unit]
+
+        @pl.loop(1, 4 * U)
+        def _(m):
+            turn_copy(ph, m).start()
+
+        lat_v[ph, :, lanes_of(x)] = jnp.concatenate([total[:, :T].T, total[:, T:].T], axis=1).astype(BF16)
+        for peer in peers:
+            fin_copy(ph, x, peer, x).start()
+
+    def turn_copy(ph, m):
+        dx = m & 3
+        there = (unit + lax.shift_right_logical(m, 2)) & (U - 1)
+        where = {"dp": (x + dx) & 3, "expert": z * U + there}
+        return remote(turned.at[ph, there], taken.at[ph, m], turn_ssem.at[ph], turn_rsem.at[ph], where)
+
+    def turn_wait(ph, sem, buf):
+        pltpu.make_async_copy(buf.at[ph, 1 : 4 * U], buf.at[ph, 1 : 4 * U], sem.at[ph]).wait()
 
     def lanes_of(q):
         return pl.ds(pl.multiple_of(q * Q, Q), Q)
 
-    def fin_copy(ph, ref, q, peer, slot):
-        src = ref.at[:, lanes_of(q)]
+    def fin_copy(ph, q, peer, slot):
+        src = lat_v.at[ph, :, lanes_of(q)]
         return remote(src, src, fin_ssem.at[ph, peer], fin_rsem.at[ph, slot], {"dp": peer})
 
-    def fin_start(ph, ref, value):
-        ref[:, lanes_of(x)] = value
+    def fin_finish(ph):
         for peer in peers:
-            fin_copy(ph, ref, x, peer, x).start()
-
-    def fin_finish(ph, ref):
-        for peer in peers:
-            fin_copy(ph, ref, peer, peer, peer).wait_recv()
+            fin_copy(ph, peer, peer, peer).wait_recv()
+
+    cols = Dd // 2
+
+    def col_chunk(c):
+        return slice(c * cols, (c + 1) * cols)
+
+    def z_copy(ph, c, step, source, target):
+        return remote(
+            zsend.at[ph, target, :, col_chunk(c)],
+            zrecv.at[ph, source, :, col_chunk(c)],
+            z_ssem.at[ph, c, step],
+            z_rsem.at[ph, c, step],
+            {"expert": at(target, y, core)},
+        )
+
+    def z_start(ph):
+        near_finish(1 - ph)
+        turn_wait(ph, turn_rsem, taken)
+        other = (go_g, tok_g)[ph]
+        left_side = jnp.concatenate(
+            [taken[ph, 4 * u : 4 * u + 4].reshape(Z * RB, T) for u in range(U)], axis=1
+        )
+        for c in range(2):
+            here = col_chunk(c)
+            right_side = other[:, :, here].reshape(U * T, cols)
+            value = jnp.dot(left_side, right_side, preferred_element_type=F32).reshape(4, 2, RB, cols)
+            for dx in range(4):
+                first = 2 * ((x + 4 - dx) & 3)
+                gsum[ph, pl.ds(first, 2), :, here] = value[dx]
+                zsend[ph, pl.ds(first, 2), :, here] = value[dx].astype(BF16)
+            for step in range(1, Z):
+                z_copy(ph, c, step, z, (z + step) & (Z - 1)).start()
+
+    def z_finish(ph):
+        for c in range(2):
+            here = col_chunk(c)
+            total = gsum[ph, z, :, here]
+            for step in range(1, Z):
+                source = (z + Z - step) & (Z - 1)
+                z_copy(ph, c, step, source, z).wait_recv()
+                total = total + zrecv[ph, source, :, here].astype(F32)
+            gsum[ph, z, :, here] = total * scaling
+        store(gsum.at[ph, z], (gfl_out, gtl_out)[ph])
 
     stores = []
 
@@ -436,7 +583,8 @@
         copy.start()
         stores.append(copy)
 
-    fin_start(0, mixed_v, combine(0, (pph, ppl)))
+    near_forward(1)
+    combine(0, (pph, ppl))
 
     @pl.loop(0, 4)
     def _(j):
@@ -444,29 +592,44 @@
         block = full[0, j]
         gg_v[rows, :] = (lax.dot_general(block, gpg_v[...], FIRST, preferred_element_type=F32) * scaling).astype(BF16)
         gu_v[rows, :] = (lax.dot_general(block, gpu_v[...], FIRST, preferred_element_type=F32) * scaling).astype(BF16)
+
+    store(gg_v, gg_out.at[0])
+    store(gu_v, gu_out.at[0])
+    near_forward(0)
+    fin_finish(0)
+    lo_v[...] = jnp.dot(lat_v[0], fl_v[...], preferred_element_type=F32).astype(BF16)
+    store(lo_v, lo_out)
+    z_start(0)
+
+    @pl.loop(0, 4)
+    def _(j):
+        rows = pl.ds(pl.multiple_of(j * Q, Q), Q)
         gd_v[:, rows] = (
             lax.dot_general(hid_v[...], full[1, j], FIRST, preferred_element_type=F32) * scaling
         ).astype(BF16)
 
-    store(gg_v, gg_out.at[0])
-    store(gu_v, gu_out.at[0])
     store(gd_v, gd_out.at[0])
-    fin_start(1, glat_v, combine(1, (pp,)))
-    fin_finish(0, mixed_v)
-    store(mixed_v, mixed_out)
-    lo_v[...] = jnp.dot(mixed_v[...], fl_v[...], preferred_element_type=F32).astype(BF16)
-    store(lo_v, lo_out)
-    fin_finish(1, glat_v)
-    store(glat_v, glat_out)
-    gt_v[...] = lax.dot_general(glat_v[...], tl_v[...], LAST, preferred_element_type=F32).astype(BF16)
+    combine(1, (pp,))
+    z_finish(0)
+    z_start(1)
+    fin_finish(1)
+    gt_v[...] = lax.dot_general(lat_v[1], tl_v[...], LAST, preferred_element_type=F32).astype(BF16)
     store(gt_v, gt_out)
+    z_finish(1)
 
     for ph in range(2):
         for peer in peers:
             xs_copy(ph, peer).wait_send()
-        fin_ref = (mixed_v, glat_v)[ph]
+        for dy in range(Y):
+            sib_copy(ph, dy).wait_send()
+        for dy in range(1, Y):
+            near_copy(ph, dy).wait_send()
         for peer in peers:
-            fin_copy(ph, fin_ref, x, peer, x).wait_send()
+            fin_copy(ph, x, peer, x).wait_send()
+        turn_wait(ph, turn_ssem, taken)
+        for c in range(2):
+            for step in range(1, Z):
+                z_copy(ph, c, step, z, (z + step) & (Z - 1)).wait_send()
         for buf, sem in ((outgoing.at[ph], a2a_ssem.at[ph]), (leaving.at[ph], a2a_ssem.at[2 + ph])):
             pltpu.make_async_copy(buf.at[1:n], buf.at[1:n], sem).wait()
 
@@ -482,6 +645,34 @@
 
     for copy in stores:
         copy.wait()
+
+
+def copy_kernel(count, *refs):
+    sources, targets, held = refs[:count], refs[count : 2 * count], refs[2 * count : 3 * count]
+    into, out = refs[3 * count :]
+    first = [pltpu.make_async_copy(sources[i], held[i], into.at[i]) for i in range(count)]
+    second = [pltpu.make_async_copy(held[i], targets[i], out.at[i]) for i in range(count)]
+    for copy in first:
+        copy.start()
+    for i in range(count):
+        first[i].wait()
+        second[i].start()
+    for copy in second:
+        copy.wait()
+
+
+def copied(arrays):
+    count = len(arrays)
+    any_spec = pl.BlockSpec(memory_space=pl.ANY)
+    return pl.pallas_call(
+        functools.partial(copy_kernel, count),
+        out_shape=[jax.ShapeDtypeStruct(a.shape, a.dtype) for a in arrays],
+        in_specs=[any_spec] * count,
+        out_specs=[any_spec] * count,
+        scratch_shapes=[pltpu.VMEM(a.shape, a.dtype) for a in arrays] + [pltpu.SemaphoreType.DMA((count,))] * 2,
+        compiler_params=pltpu.CompilerParams(vmem_limit_bytes=62 * 1024 * 1024),
+        cost_estimate=pl.CostEstimate(flops=0, bytes_accessed=8 * 2**20, transcendentals=0),
+    )(*arrays)
 
 
 def layer_call(capacity, n, routes, slot_index, route_gates, tokens, to_latent, from_latent, gate, up, down, grad_output):
@@ -493,7 +684,10 @@
     G = 8 if n >= 16 else 4
     NG = n // G
     NC = min(4, NG)
-    cfg = dict(n=n, T=T, R=R, L=L, Q=Q, W=W, G=G, NG=NG, NC=NC, scaling=float((T * n) ** -0.5))
+    Z, RB = 8, L // n
+    Y = n // (2 * Z)
+    U = 2 * Y
+    cfg = dict(Z=Z, Y=Y, RB=RB, Dd=Dd, n=n, T=T, R=R, L=L, Q=Q, W=W, G=G, NG=NG, NC=NC, scaling=float((T * n) ** -0.5))
     rows = n * R
     vm = lambda shape, dtype=BF16: pltpu.VMEM(shape, dtype)
     dma = lambda *shape: pltpu.SemaphoreType.DMA(shape)
@@ -505,24 +699,28 @@
         (gate.shape, BF16),
         (up.shape, BF16),
         (down.shape, BF16),
-        ((T, L), BF16),
-        ((T, L), BF16),
+        ((RB, Dd), F32),
+        ((RB, Dd), F32),
     ]
     scratch = [
-        vm((T, Dd)),
+        vm((U, T, Dd)),
         vm((Dd, L)),
         vm((L, Dd)),
         vm((L, Hs)),
         vm((L, Hs)),
         vm((Hs, L)),
-        vm((T, Dd)),
+        vm((U, T, Dd)),
         vm((T, Dd)),
         vm((T, Dd)),
         vm((L, Hs)),
         vm((L, Hs)),
         vm((Hs, L)),
-        vm((T, L)),
-        vm((T, L)),
+        vm((2, T, L)),
+        vm((2, U, 2, RB, T)),
+        vm((2, 4 * U, 2, RB, T)),
+        vm((2, Z, RB, Dd)),
+        vm((2, Z, RB, Dd)),
+        vm((2, Z, RB, Dd), F32),
         vm((2, 4, T, Q)),
         vm((2, 4, T, Q)),
         vm((n, T), jnp.int32),
@@ -556,6 +754,16 @@
         dma(2, NC, 6),
         dma(2, 4),
         dma(2, 4),
+        dma(2, Y),
+        dma(2, Y),
+        dma(2, Y),
+        dma(2, Y),
+        dma(2),
+        dma(2),
+        dma(2, 2, Z),
+        dma(2, 2, Z),
+        pltpu.SemaphoreType.REGULAR,
+        pltpu.SemaphoreType.REGULAR,
     ]
     flops = 2 * rows * L * Hs * 9 + 2 * T * L * Dd * 4
     return pl.pallas_call(
@@ -569,15 +777,6 @@
         ),
         cost_estimate=pl.CostEstimate(flops=flops, bytes_accessed=16 * 2**20, transcendentals=rows * Hs),
     )(routes.T, slot_index.T, route_gates.T, tokens, to_latent, from_latent, gate, up, down, grad_output)
-
-
-def spread_grad(left_side, right_side, scaling):
-    return lax.psum_scatter(
-        lax.dot_general(left_side, right_side, FIRST, preferred_element_type=F32) * scaling,
-        "expert",
-        scatter_dimension=0,
-        tiled=True,
-    )
 
 
 def local(
@@ -602,8 +801,7 @@
             5 * token_count * route_count // (4 * expert_count * dp_count),
         ),
     )
-    scaling = (token_count * expert_count) ** (-0.5)
-    layer_output, grad_tokens, grad_gate, grad_up, grad_down, mixed, grad_latent = layer_call(
+    results = layer_call(
         capacity,
         expert_count,
         routes,
@@ -617,8 +815,7 @@
         expert_down,
         grad_output,
     )
-    grad_from_latent = spread_grad(mixed, grad_output, scaling)
-    grad_to_latent = spread_grad(grad_latent, tokens, scaling)
+    layer_output, grad_tokens, grad_gate, grad_up, grad_down, grad_to_latent, grad_from_latent = copied(results)
     return (
         layer_output,
         grad_tokens,

time: 450 us -> 152 us (0.34)
  waiting for transfers between devices: 279 us -> 0 us
  between operations: 14.1 us -> 0.64 us
  Pallas kernels: 140 us -> 151 us
  matrix products: 6.38 us -> 0 us
  local copies, waits for them, and re-layouts: 5.31 us -> 0 us
    reduce_scatter x2 -> x0, waiting for transfers between devices: 279 us -> none  [spread_grad(): lax.psum_scatter(lax.dot_general(left_side, right_side, FIRST, preferred_...]
    pallas_call x1, Pallas kernels: 140 us -> 148 us  [layer_call(): pl.pallas_call(functools.partial(layer_kernel, cfg), out_shape=[jax.Shape...]
    dot_general x2 -> x0, matrix products: 6.38 us -> none  [spread_grad(): lax.dot_general(left_side, right_side, FIRST, preferred_element_type=F32)]
    unnamed x19 -> x0, local copies, waits for them, and re-layouts: 5.31 us -> none
  transfers between devices with their start and end apart: 2 -> 0, of which waited for: 2 -> 0; matrix products, arithmetic and copies ran while one was open for 1% -> 0% of each run, Pallas kernels for 0% -> 0%
where the time goes in v3:
time: 152 us
  Pallas kernels  151 us (99%)
    pallas_call x1, Pallas kernels, layer_call(): pl.pallas_call(functools.partial(layer_kernel, cfg), out_shape=[jax.Shape...  148 us
    pallas_call x1, Pallas kernels, copied(): pl.pallas_call(functools.partial(copy_kernel, count), out_shape=[jax.Shap...  3.33 us

profile of v3, /device:TPU:1, one launch (start us, length us, event | category | flops | bytes accessed | tf_op | source)
XLA Modules:
  0.0 151.6 jit_solution(10152549267948038877)
XLA Ops:
  0.6 147.6 %shard_map.153 = (bf16[128,1024]{1,0:T(8,128)(2,1)}, bf16[128,1024]{1,0:T(8,128)(2,1)}, bf16[1,1024,512]{2,1,0:T(8,128)(2,1)}, bf16[1,1024,512]{2,1,0:T(8,128)(2...) custom-call(s32[8,128]{1,0:T(8,128)} %bitcast.3, s32[8,128]{1,0:T(8,128)} %bitcast.4, ...), custom_call_target="tpu_custom_call" | custom-call | flops 13153337344 | bytes 16777216 | tf_op jit(solution)/shard_map/pallas_call | solution.py:769
  148.3 3.3 %shard_map.154 = (bf16[128,1024]{1,0:T(8,128)(2,1)}, bf16[128,1024]{1,0:T(8,128)(2,1)}, bf16[1,1024,512]{2,1,0:T(8,128)(2,1)}, bf16[1,1024,512]{2,1,0:T(8,128)(2...) custom-call(bf16[128,1024]{1,0:T(8,128)(2,1)} %get-tuple-element.21.refs_0_, ...), custom_call_target="tpu_custom_call" | custom-call | bytes 8388608 | tf_op jit(solution)/shard_map/pallas_call | solution.py:667

commit v4 on v3

--- a/solution.py
+++ b/solution.py
@@ -125,11 +125,15 @@
 
     sibling = {"expert": at(z, y, 1 - core)}
 
+    unit_bits = U.bit_length() - 1
+
     def offsets(i):
-        j = i & (Z - 1)
-        u = lax.shift_right_logical(i, Z.bit_length() - 1)
-        step = lax.shift_right_logical(j + 1, 1)
-        dz = jnp.where((j & 1) == 1, step, Z - step)
+        v = i - U
+        p = lax.shift_right_arithmetic(v, unit_bits + 1) + 1
+        w = v & (2 * U - 1)
+        paired = lax.shift_right_logical(w, 1)
+        dz = jnp.where(v < 0, 0, jnp.where((p < Z // 2) & ((w & 1) == 1), Z - p, p))
+        u = jnp.where(v < 0, i, jnp.where(p < Z // 2, paired, w))
         return dz, lax.shift_right_logical(u, 1), u & 1
 
     def target_of(i):
@@ -234,31 +238,34 @@
 
     r_iota = lax.broadcasted_iota(jnp.int32, (G, R2, T), 1)
 
-    @pl.loop(0, NG)
-    def _(g):
-        ks = pl.ds(pl.multiple_of(g * G, G), G)
-        rows = pl.ds(pl.multiple_of(g * G * R2, G * R2), G * R2)
-        s8 = jnp.broadcast_to(s_tab[ks, :].reshape(G, 1, T), (G, R2, T))
-        g8 = jnp.broadcast_to(g_tab[ks, :].reshape(G, 1, T), (G, R2, T))
-        g_hi = g8.astype(BF16).astype(F32)
-        g_lo = g8 - g_hi
-        for h in range(2):
-            match = s8 == r_iota - h * R
-            lanes = slice(h * T, (h + 1) * T)
-            pp[rows, lanes] = jnp.where(match, 1.0, 0.0).reshape(G * R2, T).astype(BF16)
-            pph[rows, lanes] = jnp.where(match, g_hi, 0.0).reshape(G * R2, T).astype(BF16)
-            ppl[rows, lanes] = jnp.where(match, g_lo, 0.0).reshape(G * R2, T).astype(BF16)
+    def spread_table(table, ks):
+        return jnp.broadcast_to(table[ks, :].reshape(G, 1, T), (G, R2, T))
 
     def dispatch(ph, stacked):
         @pl.loop(0, NG)
         def _(g):
             ks = pl.ds(pl.multiple_of(g * G, G), G)
             rows = pl.ds(pl.multiple_of(g * G * R2, G * R2), G * R2)
+            s8 = spread_table(s_tab, ks)
+            matches = [s8 == r_iota - h * R for h in range(2)]
+
+            def one_hot(value):
+                return jnp.concatenate(
+                    [jnp.where(match, value, 0.0).reshape(G * R2, T).astype(BF16) for match in matches], axis=1
+                )
+
             if ph == 0:
-                block = jnp.dot(pp[rows, :], stacked, preferred_element_type=F32)
+                weight = one_hot(1.0)
+                pp[rows, :] = weight
+                block = jnp.dot(weight, stacked, preferred_element_type=F32)
             else:
-                block = jnp.dot(pph[rows, :], stacked, preferred_element_type=F32)
-                block = block + jnp.dot(ppl[rows, :], stacked, preferred_element_type=F32)
+                g8 = spread_table(g_tab, ks)
+                g_hi = g8.astype(BF16).astype(F32)
+                high, low = one_hot(g_hi), one_hot(g8 - g_hi)
+                pph[rows, :] = high
+                ppl[rows, :] = low
+                block = jnp.dot(high, stacked, preferred_element_type=F32)
+                block = block + jnp.dot(low, stacked, preferred_element_type=F32)
             outgoing[ph, ks] = block.reshape(G, R2, W).astype(BF16)
 
             @pl.loop(jnp.maximum(g * G, 1), g * G + G)
@@ -276,7 +283,6 @@
     latent_rows = xs_finish(0)
     pl.semaphore_wait(core_ready, 1)
     dispatch(0, latent_rows)
-    dispatch(1, xs_finish(1))
 
     def sib_copy(i, dy):
         ref = (tok_g, go_g)[i]
@@ -312,8 +318,6 @@
         for dy in range(Y):
             sib_wait(i, dy)
 
-    near_start(1)
-    near_start(0)
 
     def a2a_wait(ph, buf, g):
         @pl.when(g == 0)
@@ -437,15 +441,21 @@
         value = lax.dot_general(grad_gate, gate_v[...], LAST, preferred_element_type=F32)
         return value + lax.dot_general(grad_up, up_v[...], LAST, preferred_element_type=F32)
 
-    @pl.loop(0, NG)
+    grad_rows = xs_finish(1)
+    ag_start(0, 0)
+    dispatch(1, grad_rows)
+
+    near_start(1)
+    near_start(0)
+
+    @pl.loop(1, NG)
     def _(g):
         ag_start(0, g)
 
-        @pl.when(g > 0)
+        @pl.when(g > 1)
         def _():
-            ag_forward(0, g - 1)
-
-    ag_forward(0, NG - 1)
+            ag_forward(0, g - 2)
+
     for load in loads[4:]:
         load.wait()
 
@@ -455,9 +465,13 @@
             g = c * GC + i
             ag_start(1, g)
 
-            @pl.when(g > 0)
+            @pl.when(g > 1)
             def _():
-                ag_forward(1, g - 1)
+                ag_forward(1, g - 2)
+
+            @pl.when(g <= 1)
+            def _():
+                ag_forward(0, NG - 2 + g)
 
         for i in range(GC):
             ag_finish(0, c * GC + i)
@@ -467,31 +481,25 @@
         def _():
             rs_relay(0, c - 1)
 
+    ag_forward(1, NG - 2)
     ag_forward(1, NG - 1)
     rs_relay(0, NC - 1)
 
     @pl.loop(0, NC)
-    def _(c):
+    def _(step):
+        c = NC - 1 - step
         for i in range(GC):
             ag_finish(1, c * GC + i)
         rs_start(1, c, bwd(c))
-        rs_finish(0, c)
-
-        @pl.when(c > 0)
-        def _():
-            rs_relay(1, c - 1)
-
-    rs_relay(1, NC - 1)
+        rs_finish(0, step)
+
     returned[0, 0] = leaving[0, 0]
-
-    @pl.loop(0, NC)
-    def _(c):
-        rs_finish(1, c)
-
-    returned[1, 0] = leaving[1, 0]
-
-    def combine(ph, weights):
-        def step(g, total):
+    near_forward(0)
+    near_forward(1)
+
+    def combine(ph, weights, order):
+        def step(i, total):
+            g = order(i)
             a2a_wait(2 + ph, returned.at[ph], g)
             ks = pl.ds(pl.multiple_of(g * G, G), G)
             rows = pl.ds(pl.multiple_of(g * G * R2, G * R2), G * R2)
@@ -583,33 +591,43 @@
         copy.start()
         stores.append(copy)
 
-    near_forward(1)
-    combine(0, (pph, ppl))
-
-    @pl.loop(0, 4)
-    def _(j):
-        rows = pl.ds(pl.multiple_of(j * Q, Q), Q)
-        block = full[0, j]
-        gg_v[rows, :] = (lax.dot_general(block, gpg_v[...], FIRST, preferred_element_type=F32) * scaling).astype(BF16)
-        gu_v[rows, :] = (lax.dot_general(block, gpu_v[...], FIRST, preferred_element_type=F32) * scaling).astype(BF16)
-
+    def grad_in(first, last):
+        @pl.loop(first, last)
+        def _(j):
+            rows = pl.ds(pl.multiple_of(j * Q, Q), Q)
+            block = full[0, j]
+            for weight, result in ((gpg_v, gg_v), (gpu_v, gu_v)):
+                value = lax.dot_general(block, weight[...], FIRST, preferred_element_type=F32)
+                result[rows, :] = (value * scaling).astype(BF16)
+
+    def grad_back(first, last):
+        @pl.loop(first, last)
+        def _(j):
+            rows = pl.ds(pl.multiple_of(j * Q, Q), Q)
+            value = lax.dot_general(hid_v[...], full[1, j], FIRST, preferred_element_type=F32)
+            gd_v[:, rows] = (value * scaling).astype(BF16)
+
+    rs_relay(1, NC - 1)
+    grad_in(0, 2)
+    for c in range(NC - 2, -1, -1):
+        rs_relay(1, c)
+        if c == NC - 2:
+            grad_in(2, 4)
+        if c > 0:
+            rs_finish(1, c + 1)
+    combine(0, (pph, ppl), lambda i: i)
+    rs_finish(1, 1)
+    rs_finish(1, 0)
+    returned[1, 0] = leaving[1, 0]
     store(gg_v, gg_out.at[0])
     store(gu_v, gu_out.at[0])
-    near_forward(0)
     fin_finish(0)
     lo_v[...] = jnp.dot(lat_v[0], fl_v[...], preferred_element_type=F32).astype(BF16)
     store(lo_v, lo_out)
     z_start(0)
-
-    @pl.loop(0, 4)
-    def _(j):
-        rows = pl.ds(pl.multiple_of(j * Q, Q), Q)
-        gd_v[:, rows] = (
-            lax.dot_general(hid_v[...], full[1, j], FIRST, preferred_element_type=F32) * scaling
-        ).astype(BF16)
-
+    combine(1, (pp,), lambda i: NG - 1 - i)
+    grad_back(0, 4)
     store(gd_v, gd_out.at[0])
-    combine(1, (pp,))
     z_finish(0)
     z_start(1)
     fin_finish(1)

time: 152 us -> 148 us (0.974)
  Pallas kernels: 151 us -> 147 us
    pallas_call x1, Pallas kernels: 148 us -> 143 us  [layer_call(): pl.pallas_call(functools.partial(layer_kernel, cfg), out_shape=[jax.Shape...]
where the time goes in v4:
time: 148 us; the launch traced here: 147 us
  Pallas kernels  147 us (99%)
    pallas_call x1, Pallas kernels, layer_call(): pl.pallas_call(functools.partial(layer_kernel, cfg), out_shape=[jax.Shape...  143 us
    pallas_call x1, Pallas kernels, copied(): pl.pallas_call(functools.partial(copy_kernel, count), out_shape=[jax.Shap...  3.33 us

profile of v4, /device:TPU:1, one launch (start us, length us, event | category | flops | bytes accessed | tf_op | source)
XLA Modules:
  0.0 147.5 jit_solution(11897501020743576558)
XLA Ops:
  0.6 143.5 %shard_map.153 = (bf16[128,1024]{1,0:T(8,128)(2,1)}, bf16[128,1024]{1,0:T(8,128)(2,1)}, bf16[1,1024,512]{2,1,0:T(8,128)(2,1)}, bf16[1,1024,512]{2,1,0:T(8,128)(2...) custom-call(s32[8,128]{1,0:T(8,128)} %bitcast.3, s32[8,128]{1,0:T(8,128)} %bitcast.4, ...), custom_call_target="tpu_custom_call" | custom-call | flops 13153337344 | bytes 16777216 | tf_op jit(solution)/shard_map/pallas_call | solution.py:787
  144.1 3.3 %shard_map.154 = (bf16[128,1024]{1,0:T(8,128)(2,1)}, bf16[128,1024]{1,0:T(8,128)(2,1)}, bf16[1,1024,512]{2,1,0:T(8,128)(2,1)}, bf16[1,1024,512]{2,1,0:T(8,128)(2...) custom-call(bf16[128,1024]{1,0:T(8,128)(2,1)} %get-tuple-element.21.refs_0_, ...), custom_call_target="tpu_custom_call" | custom-call | bytes 8388608 | tf_op jit(solution)/shard_map/pallas_call | solution.py:685

commit v5 on v4

--- a/solution.py
+++ b/solution.py
@@ -231,7 +231,6 @@
     loads[3].wait()
     for load in loads[4:]:
         load.start()
-    xs_start(1, lax.dot_general(go_g[0], fl_v[...], LAST, preferred_element_type=F32))
     if Y > 1:
         pl.semaphore_wait(y_ready, Y - 1)
     signal(core_ready, sibling)
@@ -283,6 +282,7 @@
     latent_rows = xs_finish(0)
     pl.semaphore_wait(core_ready, 1)
     dispatch(0, latent_rows)
+    xs_start(1, lax.dot_general(go_g[0], fl_v[...], LAST, preferred_element_type=F32))
 
     def sib_copy(i, dy):
         ref = (tok_g, go_g)[i]

time: 148 us -> 147 us (level)
  no operation moved by 1% of the time
where the time goes in v5:
time: 147 us
  Pallas kernels  147 us (100%)
    pallas_call x1, Pallas kernels, layer_call(): pl.pallas_call(functools.partial(layer_kernel, cfg), out_shape=[jax.Shape...  143 us
    pallas_call x1, Pallas kernels, copied(): pl.pallas_call(functools.partial(copy_kernel, count), out_shape=[jax.Shap...  3.33 us

profile of v5, /device:TPU:1, one launch (start us, length us, event | category | flops | bytes accessed | tf_op | source)
XLA Modules:
  0.0 147.3 jit_solution(2363182368027726733)
XLA Ops:
  0.6 143.3 %shard_map.153 = (bf16[128,1024]{1,0:T(8,128)(2,1)}, bf16[128,1024]{1,0:T(8,128)(2,1)}, bf16[1,1024,512]{2,1,0:T(8,128)(2,1)}, bf16[1,1024,512]{2,1,0:T(8,128)(2...) custom-call(s32[8,128]{1,0:T(8,128)} %bitcast.3, s32[8,128]{1,0:T(8,128)} %bitcast.4, ...), custom_call_target="tpu_custom_call" | custom-call | flops 13153337344 | bytes 16777216 | tf_op jit(solution)/shard_map/pallas_call | solution.py:787
  143.9 3.3 %shard_map.154 = (bf16[128,1024]{1,0:T(8,128)(2,1)}, bf16[128,1024]{1,0:T(8,128)(2,1)}, bf16[1,1024,512]{2,1,0:T(8,128)(2,1)}, bf16[1,1024,512]{2,1,0:T(8,128)(2...) custom-call(bf16[128,1024]{1,0:T(8,128)(2,1)} %get-tuple-element.21.refs_0_, ...), custom_call_target="tpu_custom_call" | custom-call | bytes 8388608 | tf_op jit(solution)/shard_map/pallas_call | solution.py:685
